TPU v7x, 128 devices: a whole 4x4x4 slice. The times are simulated.
128 devices in a mesh: expert: 2 (over z_lo), group: 4 (over z_hi, core), seq: 16 (over x, y).
Axes of the slice: x: 4, y: 4, z: 4 (z_hi: 2, z_lo: 2; z = z_hi * 2 + z_lo), core: 2. Of those that a mesh axis runs over, the one named last changes fastest.
Arguments:
- latent: bfloat16 [2, 4, 2048, 64], P('expert', 'group', 'seq'), may hold values from -17 to 17
- text_cache: bfloat16 [2, 4, 512, 32, 256], P('expert', 'group', None, 'seq'), may hold values from -6 to 6
- patch_weight: bfloat16 [2, 64, 5120], P('expert'), may hold values from -0.75 to 0.75
- patch_bias: float32 [2, 5120], P('expert'), may hold values from -3 to 3
- qkv_weight: bfloat16 [2, 5120, 3, 4096], P('expert', None, None, 'seq'), may hold values from -0.10062306 to 0.10062306
- qk_gain: float32 [2, 2, 4096], P('expert', None, 'seq'), may hold values from 0.6 to 5
- modulation: float32 [2, 40, 2, 5120], P('expert'), may hold values from -2.5 to 2.5
- step_index: int32 [2, 4], replicated, may hold values from 0 to 39
- lengths: int32 [2, 4], replicated, may hold values from 512 to 2048, as said below
- crossing: int32 [2, 2], replicated, may hold values from 0 to 3, as said below
Outputs:
- attended: bfloat16 [2, 4, 2048, 4096], P('expert', 'group', 'seq')
- cache_after: bfloat16 [2, 4, 512, 32, 256], P('expert', 'group', None, 'seq')
Inputs may be any that keep to these rules, and one draw needn't show every extreme that they name: `crossing`: sources are distinct and destinations are distinct. `lengths`: some slot has exactly 2048.
All inputs are finite; a program needn't handle non-finite values.
Results may differ from a plain program's by a relative error of at most 0.0056.
Values may be sent and summed in bfloat16 or wider, within the bound.
A program may use at most 128 MiB of HBM per device.

v0:
```python
import jax
import jax.numpy as jnp
from jax import lax
from jax.sharding import PartitionSpec as P

HD = 128


norm_eps = 1e-06
masked_score = -1e30


def shards(
    latent,
    text_cache,
    patch_weight,
    patch_bias,
    qkv_weight,
    qk_gain,
    modulation,
    step_index,
    lengths,
    crossing,
):
    groups = lax.axis_size("group")
    expert_id = lax.axis_index("expert")
    group_id = lax.axis_index("group")
    dest_hit = crossing[:, 1] == group_id
    source_hit = crossing[:, 0] == group_id
    arrived = jnp.logical_and(expert_id == 1, jnp.any(dest_hit))
    vacated = jnp.logical_and(expert_id == 0, jnp.any(source_hit))
    source_group = jnp.sum(jnp.where(dest_hit, crossing[:, 0], 0))
    step_now = jnp.where(arrived, step_index[0, source_group], step_index[expert_id, group_id])
    length_now = jnp.where(
        vacated, 0, jnp.where(arrived, lengths[0, source_group], lengths[expert_id, group_id])
    )
    own_rows = latent[0, 0]
    own_cache = text_cache[0, 0]
    slot_count = 2 * groups
    target = groups + jnp.sum(jnp.where(source_hit, crossing[:, 1], 0))
    sending = jnp.logical_and(expert_id == 0, jnp.any(source_hit))
    chosen = jnp.logical_and(sending, jnp.arange(slot_count) == target)
    outbound = (
        jnp.where(chosen[:, None, None], own_rows[None], jnp.zeros_like(own_rows)[None]),
        jnp.where(chosen[:, None, None, None], own_cache[None], jnp.zeros_like(own_cache)[None]),
    )
    inbound = (
        lax.all_to_all(outbound[0], ("expert", "group"), split_axis=0, concat_axis=0, tiled=True),
        lax.all_to_all(outbound[1], ("expert", "group"), split_axis=0, concat_axis=0, tiled=True),
    )
    moved_rows = lax.dynamic_index_in_dim(inbound[0], source_group, 0, keepdims=False)
    moved_cache = lax.dynamic_index_in_dim(inbound[1], source_group, 0, keepdims=False)
    slot_rows = jnp.where(arrived, moved_rows, own_rows)
    slot_cache = jnp.where(arrived, moved_cache, own_cache)
    slot_cache = jnp.where(vacated, jnp.zeros_like(slot_cache), slot_cache)
    modulate = lax.dynamic_index_in_dim(modulation[0], step_now, 0, keepdims=False)
    values = (
        jnp.dot(slot_rows, patch_weight[0], preferred_element_type=jnp.float32)
        + patch_bias[0][None, :]
    )
    centre = jnp.mean(values, axis=-1, keepdims=True)
    spread = jnp.mean(jnp.square(values - centre), axis=-1, keepdims=True)
    normed = (
        (values - centre) * lax.rsqrt(spread + norm_eps) * (1.0 + modulate[1]) + modulate[0]
    ).astype(jnp.bfloat16)
    dev_width = qkv_weight.shape[3]
    model_width = qkv_weight.shape[1]
    weight_cols = qkv_weight[0].reshape(model_width, 3 * dev_width)
    projected = jnp.dot(
        lax.all_gather(normed, "seq", axis=0, tiled=True),
        weight_cols,
        preferred_element_type=jnp.float32,
    )
    seq_len = projected.shape[0]
    projected = projected.reshape(seq_len, 3, dev_width)
    queries = projected[:, 0, :]
    key_rows = projected[:, 1, :]
    partial_value = jnp.stack(
        [jnp.sum(queries * queries, axis=-1), jnp.sum(key_rows * key_rows, axis=-1)], axis=1
    )
    totals = lax.psum(partial_value, "seq")
    hw_total = dev_width * lax.axis_size("seq")
    queries = (queries * lax.rsqrt(totals[:, 0:1] / hw_total + norm_eps) * qk_gain[0, 0]).astype(
        jnp.bfloat16
    )
    key_rows = (key_rows * lax.rsqrt(totals[:, 1:2] / hw_total + norm_eps) * qk_gain[0, 1]).astype(
        jnp.bfloat16
    )
    value_rows = projected[:, 2, :].astype(jnp.bfloat16)
    heads_here = dev_width // HD
    score_scale = 1.0 / HD**0.5
    live_keys = jnp.arange(seq_len, dtype=jnp.int32) < length_now
    keys_three = key_rows.reshape(seq_len, heads_here, HD)
    values_three = value_rows.reshape(seq_len, heads_here, HD)
    block_rows = min(512, seq_len)
    block_count = seq_len // block_rows
    query_blocks = queries.reshape(block_count, block_rows, heads_here, HD)

    def attend(block_query):
        scores = (
            jnp.einsum("qhd,khd->hqk", block_query, keys_three, preferred_element_type=jnp.float32)
            * score_scale
        )
        scores = jnp.where(live_keys[None, None, :], scores, masked_score)
        row_max = jnp.max(scores, axis=-1, keepdims=True)
        weights = jnp.exp(scores - row_max)
        probabilities = (weights / jnp.sum(weights, axis=-1, keepdims=True)).astype(jnp.bfloat16)
        return jnp.einsum(
            "hqk,khd->qhd", probabilities, values_three, preferred_element_type=jnp.float32
        )

    head_output = lax.map(attend, query_blocks).reshape(seq_len, dev_width)
    head_output = jnp.where(live_keys[:, None], head_output, 0.0).astype(jnp.bfloat16)
    attended = lax.all_to_all(head_output, "seq", split_axis=0, concat_axis=1, tiled=True)
    return (attended[None, None], slot_cache[None, None])


def solution(mesh):
    in_specs = (
        P("expert", "group", "seq", None),
        P("expert", "group", None, "seq", None),
        P("expert", None, None),
        P("expert", None),
        P("expert", None, None, "seq"),
        P("expert", None, "seq"),
        P("expert", None, None, None),
        P(),
        P(),
        P(),
    )
    out_specs = (P("expert", "group", "seq", None), P("expert", "group", None, "seq", None))
    return jax.shard_map(shards, mesh=mesh, in_specs=in_specs, out_specs=out_specs, check_vma=False)
```

profile of v0, /device:TPU:32, one launch (start us, length us, event | category | flops | bytes accessed | tf_op | source)
XLA Modules:
  0.0 350.3 jit_solution(9153570916432929869)
XLA Ops:
  7.2 0.0 copy-start
  7.2 1.0 slice_reduce_fusion
  8.2 0.6 compare_reduce_fusion.1
  8.8 0.7 fusion.42
  10.9 1.5 broadcast_select_fusion.3
  12.3 5.4 %all-to-all-start = ((bf16[8,128,64]{1,2,0:T(8,128)(2,1)}), bf16[8,128,64]{1,2,0:T(8,128)(2,1)S(1)}, u32[]{:S(2)}, u32[]{:S(2)}) async-start(bf16[8,128,64]{1,2,0:T(8,128)(2,1)} %broadcast_select_fusion.3), calls=%async_computation | async-start | bytes 262144 | tf_op jit(solution)/shard_map/all_to_all | solution.py:48
  17.7 0.0 all-gather.2.cloned.1.call-start
  17.8 0.7 compare_reduce_fusion
  21.1 1.4 fusion.49
  23.8 0.9 dynamic-slice_add_fusion
  26.0 0.0 all-to-all-done
  26.0 0.0 copy-done
  26.0 1.4 fusion.51
  27.4 0.4 multiply_reduce_fusion
  27.8 0.0 copy-start.3
  27.8 1.6 add_convert_fusion
  29.4 0.0 all-gather.2.cloned.1.call-update
  29.4 0.0 copy-done.3
  29.4 5.6 %broadcast_select_fusion = bf16[8,512,2,256]{3,2,1,0:T(2,128)(2,1)} fusion(pred[8]{0:T(512)(128)(4,1)S(1)} %compare_and_fusion, bf16[512,2,256]{2,1,0:T(2,128)(2,1)S(1)} %bitcast.81), kind=kLoop, calls=%fused_computation.25 | loop fusion | flops 2097152 | bytes 4718600 | tf_op jit(solution)/shard_map/jit(_where)/select_n | solution.py:45
  35.1 4.8 %all-to-all-start.2 = ((bf16[8,512,2,256]{3,2,1,0:T(2,128)(2,1)}), bf16[8,512,2,256]{3,2,1,0:T(2,128)(2,1)}, u32[]{:S(2)}, u32[]{:S(2)}) async-start(bf16[8,512,2,256]{3,2,1,0:T(2,128)(2,1)} %broadcast_select_fusion), calls=%async_computation.2 | async-start | bytes 8388608 | tf_op jit(solution)/shard_map/all_to_all | solution.py:49
  39.9 0.0 copy-start.6
  39.9 10.9 %copy.20 = bf16[1,5120,3,256]{1,3,2,0:T(8,128)(2,1)} copy(bf16[1,5120,3,256]{3,1,2,0:T(8,128)(2,1)} %param.16) | data formatting | bytes 15728640 | tf_op args[4]
  52.1 0.0 copy-done.6
  52.1 111.4 %all-gather.2.cloned.1.call-done = bf16[2048,5120]{1,0:T(8,128)(2,1)} async-done(((bf16[128,5120]{1,0:T(8,128)(2,1)}), bf16[2048,5120]{1,0:T(8,128)(2,1)}) %all-gather.2.cloned.1.call-update) | async-done | bytes 20971536 | tf_op jit(solution)/shard_map/all_gather | solution.py:70
  163.6 20.4 %fusion.28 = f32[2048,3,256]{0,2,1:T(8,128)S(1)} fusion(bf16[2048,5120]{1,0:T(8,128)(2,1)} %all-gather.2.cloned.1.call-done, bf16[1,5120,3,256]{1,3,2,0:T(8,128)(2,1)} %copy.20), kind=kOutput, calls=%fused_computation.23 | convolution fusion | flops 16106127360 | bytes 35127296 | tf_op jit(solution)/shard_map/dot_general | solution.py:69
  184.0 2.6 multiply_reduce_fusion.2
  186.6 1.1 slice.71
  187.7 72.4 %psum.7 = f32[2048,2]{0,1:T(2,128)S(1)} all-reduce(f32[2048,2]{0,1:T(2,128)S(1)} %pad_maximum_fusion), channel_id=1, replica_groups=mesh['expert'=2,'group'=4,'seq'=16] {'seq'}, use_global_device_ids=true, to_apply=%region_8.9 | all-reduce | flops 4096 | bytes 32768 | tf_op jit(solution)/shard_map/psum | solution.py:81
  260.1 1.9 copy.22
  262.1 3.6 %squeeze.56 = f32[4,512,2,128]{1,0,3,2:T(4,128)} reshape(f32[2048,1,256]{0,2,1:T(8,128)} %get-tuple-element.91) | data formatting | bytes 4194304 | tf_op jit(solution)/shard_map/squeeze | solution.py:76
  265.7 3.0 copy.21
  268.7 2.3 copy.23
  271.0 0.0 copy-start.2
  271.0 1.4 multiply_convert_fusion
  272.4 0.0 copy-start.4
  272.4 0.0 copy-start.5
  272.4 0.6 copy-done.2
  272.9 1.3 multiply_convert_fusion.1
  274.2 0.0 copy-done.4
  274.3 0.0 copy-done.5
  274.3 48.7 %while.11 = (s32[]{:T(128)}, bf16[4,512,2,128]{3,2,1,0:T(2,128)(2,1)S(1)}, bf16[4,512,2,128]{3,1,2,0:T(8,128)(2,1)}, bf16[2048,2,128]{2,0,1:T(8,128)(2,1)}, bf16...) while((s32[]{:T(128)}, bf16[4,512,2,128]{3,2,1,0:T(2,128)(2,1)S(1)}, ...), condition=%wide.region_12.13_spmd.clone, body=%wide.region_9.12_spmd.clone.sunk | while | flops 1086328832 | bytes 19935828 | solution.py:112
  274.3 7.2 %fusion.63 = (f32[2,512]{1,0:T(2,128)S(1)}, f32[2,512,2048]{2,1,0:T(8,128)}) fusion(pred[2048]{0:T(1024)(128)(4,1)S(1)} %iota_compare_fusion.2, bf16[2048,2,128]{2,0,1:T(8,128)(2,1)} %get-tuple-element.164, bf16[4,512,2,128]{3,1,2,0:T(8,128)(2,1)} %get-tuple-element.163, s32[]{:T(128)} %get-tuple-element.154), kind=kOutput, calls=%fused_computation.69.clone.1 | convolution fusion | flops 545261568 | bytes 9705984 | tf_op jit(solution)/shard_map/while/body/eval_jaxpr/sub | solution.py:106
  281.4 4.7 %fusion.64 = bf16[1,512,2,128]{3,1,2,0:T(8,128)(2,1)S(1)} fusion(bf16[2048,2,128]{2,0,1:T(8,128)(2,1)S(1)} %get-tuple-element.165, f32[2,512,2048]{2,1,0:T(8,128)} %get-tuple-element.145, f32[2,512]{1,0:T(2,128)S(1)} %get-tuple-element.146), kind=kOutput, calls=%fused_computation.10.clone.1 | convolution fusion | flops 541065216 | bytes 9703424 | tf_op jit(solution)/shard_map/while/body/eval_jaxpr/hqk,khd->qhd/dot_general | solution.py:108
  286.1 0.3 copy_dynamic-update-slice_fusion.2
  286.5 7.2 %fusion.63 = (f32[2,512]{1,0:T(2,128)S(1)}, f32[2,512,2048]{2,1,0:T(8,128)}) fusion(pred[2048]{0:T(1024)(128)(4,1)S(1)} %iota_compare_fusion.2, bf16[2048,2,128]{2,0,1:T(8,128)(2,1)} %get-tuple-element.164, bf16[4,512,2,128]{3,1,2,0:T(8,128)(2,1)} %get-tuple-element.163, s32[]{:T(128)} %get-tuple-element.154), kind=kOutput, calls=%fused_computation.69.clone.1 | convolution fusion | flops 545261568 | bytes 9705984 | tf_op jit(solution)/shard_map/while/body/eval_jaxpr/sub | solution.py:106
  293.6 4.7 %fusion.64 = bf16[1,512,2,128]{3,1,2,0:T(8,128)(2,1)S(1)} fusion(bf16[2048,2,128]{2,0,1:T(8,128)(2,1)S(1)} %get-tuple-element.165, f32[2,512,2048]{2,1,0:T(8,128)} %get-tuple-element.145, f32[2,512]{1,0:T(2,128)S(1)} %get-tuple-element.146), kind=kOutput, calls=%fused_computation.10.clone.1 | convolution fusion | flops 541065216 | bytes 9703424 | tf_op jit(solution)/shard_map/while/body/eval_jaxpr/hqk,khd->qhd/dot_general | solution.py:108
  298.3 0.3 copy_dynamic-update-slice_fusion.2
  298.6 7.2 %fusion.63 = (f32[2,512]{1,0:T(2,128)S(1)}, f32[2,512,2048]{2,1,0:T(8,128)}) fusion(pred[2048]{0:T(1024)(128)(4,1)S(1)} %iota_compare_fusion.2, bf16[2048,2,128]{2,0,1:T(8,128)(2,1)} %get-tuple-element.164, bf16[4,512,2,128]{3,1,2,0:T(8,128)(2,1)} %get-tuple-element.163, s32[]{:T(128)} %get-tuple-element.154), kind=kOutput, calls=%fused_computation.69.clone.1 | convolution fusion | flops 545261568 | bytes 9705984 | tf_op jit(solution)/shard_map/while/body/eval_jaxpr/sub | solution.py:106
  305.8 4.7 %fusion.64 = bf16[1,512,2,128]{3,1,2,0:T(8,128)(2,1)S(1)} fusion(bf16[2048,2,128]{2,0,1:T(8,128)(2,1)S(1)} %get-tuple-element.165, f32[2,512,2048]{2,1,0:T(8,128)} %get-tuple-element.145, f32[2,512]{1,0:T(2,128)S(1)} %get-tuple-element.146), kind=kOutput, calls=%fused_computation.10.clone.1 | convolution fusion | flops 541065216 | bytes 9703424 | tf_op jit(solution)/shard_map/while/body/eval_jaxpr/hqk,khd->qhd/dot_general | solution.py:108
  310.5 0.3 copy_dynamic-update-slice_fusion.2
  310.8 7.2 %fusion.63 = (f32[2,512]{1,0:T(2,128)S(1)}, f32[2,512,2048]{2,1,0:T(8,128)}) fusion(pred[2048]{0:T(1024)(128)(4,1)S(1)} %iota_compare_fusion.2, bf16[2048,2,128]{2,0,1:T(8,128)(2,1)} %get-tuple-element.164, bf16[4,512,2,128]{3,1,2,0:T(8,128)(2,1)} %get-tuple-element.163, s32[]{:T(128)} %get-tuple-element.154), kind=kOutput, calls=%fused_computation.69.clone.1 | convolution fusion | flops 545261568 | bytes 9705984 | tf_op jit(solution)/shard_map/while/body/eval_jaxpr/sub | solution.py:106
  318.0 4.7 %fusion.64 = bf16[1,512,2,128]{3,1,2,0:T(8,128)(2,1)S(1)} fusion(bf16[2048,2,128]{2,0,1:T(8,128)(2,1)S(1)} %get-tuple-element.165, f32[2,512,2048]{2,1,0:T(8,128)} %get-tuple-element.145, f32[2,512]{1,0:T(2,128)S(1)} %get-tuple-element.146), kind=kOutput, calls=%fused_computation.10.clone.1 | convolution fusion | flops 541065216 | bytes 9703424 | tf_op jit(solution)/shard_map/while/body/eval_jaxpr/hqk,khd->qhd/dot_general | solution.py:108
  322.7 0.3 copy_dynamic-update-slice_fusion.2
  323.0 0.7 reshape.97
  323.7 1.2 select_convert_fusion
  325.0 0.0 all-to-all-done.2
  325.0 3.7 %all-to-all-start.1 = ((bf16[16,128,256]{2,1,0:T(8,128)(2,1)}), bf16[16,128,256]{2,1,0:T(8,128)(2,1)S(1)}, u32[]{:S(2)}, u32[]{:S(2)}) async-start(bf16[16,128,256]{2,1,0:T(8,128)(2,1)} %select_convert_fusion), calls=%async_computation.1 | async-start | bytes 2097152 | tf_op jit(solution)/shard_map/all_to_all | solution.py:114
  328.6 0.0 copy-start.1
  328.6 2.5 broadcast_select_fusion.2
  331.1 10.3 %all-to-all-done.1 = bf16[16,128,256]{2,1,0:T(8,128)(2,1)S(1)} async-done(((bf16[16,128,256]{2,1,0:T(8,128)(2,1)}), bf16[16,128,256]{2,1,0:T(8,128)(2,1)S(1)}, u32[]{:S(2)}, u32[]{:S(2)}) %all-to-all-start.1) | async-done | bytes 1048608 | tf_op jit(solution)/shard_map/all_to_all | solution.py:114
  341.5 0.7 copy.25
  342.2 1.3 copy.26
  343.5 0.0 copy-done.1
  (13 shorter events, 0.1 us)
Async XLA Ops:
  7.2 18.8 %copy-start = (bf16[1,64,5120]{2,1,0:T(8,128)(2,1)S(1)}, bf16[1,64,5120]{2,1,0:T(8,128)(2,1)}, u32[]{:S(2)}) copy-start(bf16[1,64,5120]{2,1,0:T(8,128)(2,1)} %param.14) | copy-start | bytes 1966084
  12.3 13.7 %all-to-all-start = ((bf16[8,128,64]{1,2,0:T(8,128)(2,1)}), bf16[8,128,64]{1,2,0:T(8,128)(2,1)S(1)}, u32[]{:S(2)}, u32[]{:S(2)}) async-start(bf16[8,128,64]{1,2,0:T(8,128)(2,1)} %broadcast_select_fusion.3), calls=%async_computation | async-start | bytes 262144 | tf_op jit(solution)/shard_map/all_to_all | solution.py:48
  17.7 145.8 %all-gather.2.cloned.1.call-start = ((), (), s32[]{:S(2)}) async-start(), calls=%async_computation.3 | async-start | bytes 22282240 | tf_op jit(solution)/shard_map/all_gather | solution.py:70
  27.8 1.6 copy-start.3
  35.1 289.9 %all-to-all-start.2 = ((bf16[8,512,2,256]{3,2,1,0:T(2,128)(2,1)}), bf16[8,512,2,256]{3,2,1,0:T(2,128)(2,1)}, u32[]{:S(2)}, u32[]{:S(2)}) async-start(bf16[8,512,2,256]{3,2,1,0:T(2,128)(2,1)} %broadcast_select_fusion), calls=%async_computation.2 | async-start | bytes 8388608 | tf_op jit(solution)/shard_map/all_to_all | solution.py:49
  39.9 12.3 %copy-start.6 = (f32[1,2,256]{2,1,0:T(2,128)S(1)}, f32[1,2,256]{2,1,0:T(2,128)}, u32[]{:S(2)}) copy-start(f32[1,2,256]{2,1,0:T(2,128)} %param.17) | copy-start | bytes 6148
  271.0 2.0 copy-start.2
  272.4 1.9 copy-start.4
  272.4 1.9 copy-start.5
  325.0 16.5 %all-to-all-start.1 = ((bf16[16,128,256]{2,1,0:T(8,128)(2,1)}), bf16[16,128,256]{2,1,0:T(8,128)(2,1)S(1)}, u32[]{:S(2)}, u32[]{:S(2)}) async-start(bf16[16,128,256]{2,1,0:T(8,128)(2,1)} %select_convert_fusion), calls=%async_computation.1 | async-start | bytes 2097152 | tf_op jit(solution)/shard_map/all_to_all | solution.py:114
  328.6 14.8 %copy-start.1 = (bf16[1,64,5120]{2,1,0:T(8,128)(2,1)S(1)}, bf16[1,64,5120]{2,1,0:T(8,128)(2,1)}, u32[]{:S(2)}) copy-start(bf16[1,64,5120]{2,1,0:T(8,128)(2,1)} %param.14) | copy-start | bytes 1966084
Sparse Core Ops, SparseCore 0:
  29.5 134.0 all-gather.1
where the time goes:
time: 352 us; the launch traced here: 350 us
  waiting for transfers between devices  122 us (35%)
  blocking collectives  72.4 us (21%)
  matrix products  69.2 us (20%)
  local copies, waits for them, and re-layouts  29.7 us (8%)
  between operations  22 us (6%)
  other arithmetic  21.2 us (6%)
  starting transfers between devices  13.9 us (4%)
    all_gather x1, waiting for transfers between devices, shards(): lax.all_gather(normed, 'seq', axis=0, tiled=True)  111 us
    psum x1, blocking collectives, shards(): totals = lax.psum(partial_value, 'seq')  72.4 us
    sub x4, matrix products, attend(): weights = jnp.exp(scores - row_max)  28.7 us
    dot_general x1, matrix products, shards(): jnp.dot(lax.all_gather(normed, 'seq', axis=0, tiled=True), weight_cols, p...  20.4 us
    dot_general x4, matrix products, attend(): jnp.einsum('hqk,khd->qhd', probabilities, values_three, preferred_element...  18.7 us
    unnamed x17, local copies, waits for them, and re-layouts  15.1 us
    all_to_all x1, waiting for transfers between devices, shards(): lax.all_to_all(head_output, 'seq', split_axis=0, concat_axis=1, tiled=True)  10.3 us
  transfers between devices with their start and end apart: 4, of which 2 were waited for; matrix products, arithmetic and copies ran while one was open for 32% of the time, Pallas kernels for 0%

commit v1 on v0

v1 whole, which is shorter than its diff:
```python
import functools

import jax
import jax.numpy as jnp
from jax import lax
from jax.experimental import pallas as pl
from jax.experimental.pallas import tpu as pltpu
from jax.sharding import PartitionSpec as P

HD = 128
EPS = 1e-06
MASKED = -1e30
LOG2E = 1.4426950408889634
BF = jnp.bfloat16
F32 = jnp.float32
MESH = pl.DeviceIdType.MESH
ROWS = 80
QB = 256
KB = 256


def dot(a, b):
    return jnp.dot(a, b, preferred_element_type=F32)


def dot_nt(a, b):
    return lax.dot_general(a, b, (((1,), (1,)), ((), ())), preferred_element_type=F32)


def split(a):
    hi = a.astype(BF)
    lo = (a - hi.astype(F32)).astype(BF)
    return hi, lo


def gram(a):
    hi, lo = split(a)
    return dot_nt(hi, hi) + dot_nt(hi, lo) + dot_nt(lo, hi)


def kernel(
    n,
    crossing,
    lengths,
    steps,
    xt_ref,
    b_ref,
    gain_ref,
    p_hbm,
    mod_hbm,
    w_hbm,
    cache_hbm,
    out_hbm,
    land_hbm,
    p_v,
    mod_v,
    w_v,
    a2,
    c2,
    zin,
    xall,
    m_v,
    gbuf,
    rs_in,
    ag,
    z2,
    mt2,
    mtf,
    qaug,
    kaug,
    vaug,
    s_scr,
    p_scr,
    ostage,
    load_sem,
    zsend,
    zrecv,
    csend,
    crecv,
    fsend,
    frecv,
    xsend,
    xrecv,
    rsend,
    rrecv,
    asend,
    arecv,
    osend,
    orecv,
):
    e = lax.axis_index("expert")
    g = lax.axis_index("group")
    s = lax.axis_index("seq")
    half = lax.div(g, 2)
    core = lax.rem(g, 2)
    tokens = n * 128
    red = ROWS // 8

    ld_p = pltpu.make_async_copy(p_hbm, p_v, load_sem.at[0])
    ld_mod = pltpu.make_async_copy(mod_hbm, mod_v, load_sem.at[1])
    ld_w = [pltpu.make_async_copy(w_hbm.at[j], w_v.at[j], load_sem.at[2 + j]) for j in range(3)]
    ld_p.start()
    ld_mod.start()
    for copy in ld_w:
        copy.start()

    barrier = pltpu.get_barrier_semaphore()

    def greet(k, carry):
        pl.semaphore_signal(barrier, inc=1, device_id={"seq": lax.rem(s + k, n)}, device_id_type=MESH)
        return carry

    lax.fori_loop(1, n, greet, 0)
    for other in range(4):
        pl.semaphore_signal(
            barrier, inc=1, device_id={"expert": 1 - e, "group": other}, device_id_type=MESH
        )

    @pl.when(e == 1)
    def _():
        pl.semaphore_signal(barrier, inc=1, device_id={"group": 2 * half + 1 - core}, device_id_type=MESH)

    hit0 = crossing[0, 1] == g
    hit1 = crossing[1, 1] == g
    arrived = jnp.logical_and(e == 1, jnp.logical_or(hit0, hit1))
    source = jnp.where(hit0, crossing[0, 0], jnp.where(hit1, crossing[1, 0], 0))
    step_now = jnp.where(arrived, steps[0, source], steps[e, g])
    length = jnp.where(arrived, lengths[0, source], lengths[e, g])

    ld_p.wait()
    ld_mod.wait()
    width = p_v.shape[1]
    p_mean = jnp.mean(p_v[...].astype(F32), axis=1, keepdims=True)
    b_mean = jnp.mean(b_ref[...], axis=1, keepdims=True)
    part = 1024
    tail_row = lax.broadcasted_iota(jnp.int32, (16, part), 0)
    for i in range(width // part):
        cols = pl.ds(i * part, part)
        modulate = mod_v[step_now, :, cols]
        scale = 1.0 + modulate[1:2, :]
        shift = modulate[0:1, :]
        centred = p_v[:, cols].astype(F32) - p_mean
        bias = b_ref[:, cols] - b_mean
        bias_rows = jnp.broadcast_to(bias, (16, part))
        top = centred * scale
        bottom = jnp.where(
            tail_row == 0, bias_rows * scale, jnp.where(tail_row == 1, jnp.broadcast_to(shift, (16, part)), 0.0)
        )
        plain = jnp.where(tail_row == 0, bias_rows, 0.0)
        hi, lo = split(top)
        a2[0:64, cols] = hi
        a2[ROWS : ROWS + 64, cols] = lo
        hi, lo = split(bottom)
        a2[64:ROWS, cols] = hi
        a2[ROWS + 64 : 2 * ROWS, cols] = lo
        hi, lo = split(centred)
        c2[0:64, cols] = hi
        c2[ROWS : ROWS + 64, cols] = lo
        hi, lo = split(plain)
        c2[64:ROWS, cols] = hi
        c2[ROWS + 64 : 2 * ROWS, cols] = lo

    pl.semaphore_wait(barrier, n - 1 + 4 + e)

    def z_copy(src_group, dst_group):
        return pltpu.make_async_remote_copy(
            src_ref=xt_ref,
            dst_ref=zin.at[src_group],
            send_sem=zsend.at[dst_group],
            recv_sem=zrecv.at[src_group],
            device_id={"expert": 1, "group": dst_group},
            device_id_type=MESH,
        )

    def cache_copy(src_half, dst_half):
        return pltpu.make_async_remote_copy(
            src_ref=cache_hbm,
            dst_ref=land_hbm.at[2 * src_half + core],
            send_sem=csend.at[dst_half],
            recv_sem=crecv.at[src_half],
            device_id={"expert": 1, "group": 2 * dst_half + core},
            device_id_type=MESH,
        )

    def forward_copy(src_half, src_core):
        return pltpu.make_async_remote_copy(
            src_ref=land_hbm.at[2 * src_half + src_core],
            dst_ref=land_hbm.at[2 * src_half + src_core],
            send_sem=fsend.at[src_half],
            recv_sem=frecv.at[src_half],
            device_id={"expert": 1, "group": 2 * half + 1 - core},
            device_id_type=MESH,
        )

    @pl.when(e == 0)
    def _():
        for dst in range(4):
            z_copy(g, dst).start()
        for dst in range(2):
            cache_copy(half, dst).start()

    def project(j):
        raw = dot(a2[...], w_v[j])
        total = raw[0:ROWS, :] + raw[ROWS : 2 * ROWS, :]
        m_v[j, 0:ROWS, :] = total
        return total

    ld_w[0].wait()
    m_q = project(0)

    def x_copy(peer, slot):
        return pltpu.make_async_remote_copy(
            src_ref=xall.at[slot],
            dst_ref=xall.at[slot],
            send_sem=xsend.at[peer],
            recv_sem=xrecv.at[slot],
            device_id={"seq": peer},
            device_id_type=MESH,
        )

    @pl.when(e == 1)
    def _():
        for src in range(4):
            z_copy(src, 0).wait_recv()
        xall[s] = jnp.where(arrived, zin[source], xt_ref[...])

    @pl.when(e == 0)
    def _():
        xall[s] = xt_ref[...]

    def x_start(k, carry):
        x_copy(lax.rem(s + k, n), s).start()
        return carry

    lax.fori_loop(1, n, x_start, 0)

    ld_w[1].wait()
    m_k = project(1)
    gbuf[...] = jnp.zeros_like(gbuf)
    gbuf[:, 0:ROWS] = gram(m_q)
    gbuf[:, 128 : 128 + ROWS] = gram(m_k)

    def r_copy(peer, slot):
        return pltpu.make_async_remote_copy(
            src_ref=gbuf.at[pl.ds(pl.multiple_of(peer * 8, 8), 8)],
            dst_ref=rs_in.at[slot],
            send_sem=rsend.at[peer],
            recv_sem=rrecv.at[slot],
            device_id={"seq": peer},
            device_id_type=MESH,
        )

    def r_start(k, carry):
        peer = lax.rem(s + k, n)

        @pl.when(peer < red)
        def _():
            r_copy(peer, s).start()

        return carry

    lax.fori_loop(1, n, r_start, 0)

    var_gram = (
        dot_nt(c2[0:ROWS, :], c2[0:ROWS, :])
        + dot_nt(c2[0:ROWS, :], c2[ROWS : 2 * ROWS, :])
        + dot_nt(c2[ROWS : 2 * ROWS, :], c2[0:ROWS, :])
    ) * (1.0 / width)

    ld_w[2].wait()
    project(2)

    for j in range(3):
        m_v[j, ROWS:128, :] = jnp.zeros((128 - ROWS, 256), F32)
        full = m_v[j]
        if j < 2:
            full = full * gain_ref[j : j + 1, :]
        flipped = full.T
        hi, lo = split(flipped)
        mt2[j, :, 0:128] = hi
        mt2[j, :, 128:256] = lo
        mtf[j] = flipped

    def a_copy(peer, slot):
        return pltpu.make_async_remote_copy(
            src_ref=ag.at[slot],
            dst_ref=ag.at[slot],
            send_sem=asend.at[peer],
            recv_sem=arecv.at[slot],
            device_id={"seq": peer},
            device_id_type=MESH,
        )

    @pl.when(s < red)
    def _():
        def r_wait(k, carry):
            r_copy(0, lax.rem(s + k, n)).wait_recv()
            return carry

        lax.fori_loop(1, n, r_wait, 0)
        rs_in[s] = gbuf[pl.ds(pl.multiple_of(s * 8, 8), 8), :]
        total = rs_in[0]
        for src in range(1, n):
            total = total + rs_in[src]
        ag[s] = total

        def a_start(k, carry):
            a_copy(lax.rem(s + k, n), s).start()
            return carry

        lax.fori_loop(1, n, a_start, 0)

    def x_wait(k, carry):
        x_copy(0, lax.rem(s + k, n)).wait_recv()
        return carry

    lax.fori_loop(1, n, x_wait, 0)
    tail64 = lax.broadcasted_iota(jnp.int32, (64, 128), 0)
    ones_row = jnp.where(tail64 == 0, 1.0, 0.0).astype(BF)
    for i in range(n):
        cols = pl.ds(i * 128, 128)
        z2[0:64, cols] = xall[i]
        z2[128:192, cols] = xall[i]
        z2[64:128, cols] = ones_row
        z2[192:256, cols] = ones_row

    z0 = z2[0:128, :]
    z0f = z0.astype(F32)[0:ROWS, :]
    z80 = z0[0:ROWS, :]
    g_hi, g_lo = split(var_gram)
    t = dot(g_hi, z80) + dot(g_lo, z80)
    var = jnp.maximum(jnp.sum(t * z0f, axis=0, keepdims=True), 0.0)
    rstd = lax.rsqrt(var + EPS)

    def a_wait(k, carry):
        slot = lax.rem(s + k, n)

        @pl.when(slot < red)
        def _():
            a_copy(0, slot).wait_recv()

        return carry

    lax.fori_loop(1, n, a_wait, 0)
    both = ag[...].reshape(ROWS, 256)
    scales = []
    for j in range(2):
        g_j = both[:, j * 128 : (j + 1) * 128]
        hi, lo = split(g_j)
        t = dot(hi, z0) + dot(lo, z0)
        quad = jnp.sum(t * z0f, axis=0, keepdims=True)
        total = rstd * rstd * quad + 2.0 * rstd * t[65:66, :] + g_j[65:66, 65:66]
        scales.append(lax.rsqrt(jnp.maximum(total, 0.0) * (1.0 / (n * 256)) + EPS))
    r_q = scales[0] * (LOG2E / HD**0.5)
    r_k = scales[1]

    first16 = lax.broadcasted_iota(jnp.int32, (16, tokens), 0)
    first128 = lax.broadcasted_iota(jnp.int32, (128, tokens), 0)
    one16 = jnp.where(first16 == 0, 1.0, 0.0).astype(BF)
    one128 = jnp.where(first128 == 0, 1.0, 0.0).astype(BF)
    key_at = lax.broadcasted_iota(jnp.int32, (tokens, 128), 0)
    masks = jnp.where(key_at >= length, MASKED, 0.0).astype(BF)
    for h in range(2):
        qaug[h, 128:256, :] = one128
        vaug[h, 128:144, :] = one16
        kaug[h, :, 128:256] = masks
    piece = 512
    for i in range(tokens // piece):
        cols = slice(i * piece, (i + 1) * piece)
        rhs = z2[:, cols]
        r_i = rstd[:, cols]
        q_w = r_q[:, cols]
        k_w = r_k[:, cols]
        q_t = (dot(mt2[0], rhs) * (q_w * r_i) + mtf[0, :, 65:66] * q_w).astype(BF)
        k_t = dot(mt2[1], rhs) * (k_w * r_i) + mtf[1, :, 65:66] * k_w
        v_t = (dot(mt2[2], rhs) * r_i + mtf[2, :, 65:66]).astype(BF)
        for h in range(2):
            rows = slice(h * 128, (h + 1) * 128)
            qaug[h, 0:128, cols] = q_t[rows, :]
            vaug[h, 0:128, cols] = v_t[rows, :]
            kaug[h, cols, 0:128] = k_t[rows, :].T.astype(BF)

    blocks = tokens // QB
    mine = lax.div(s, 2)

    def o_copy(block, side, src):
        return pltpu.make_async_remote_copy(
            src_ref=ostage.at[block, pl.ds(side * 128, 128)],
            dst_ref=out_hbm.at[:, pl.ds(pl.multiple_of(src * 256, 256), 256)],
            send_sem=osend.at[2 * block + side],
            recv_sem=orecv.at[src],
            device_id={"seq": 2 * block + side},
            device_id_type=MESH,
        )

    def own_copy():
        return pltpu.make_async_copy(
            ostage.at[mine, pl.ds(pl.multiple_of((s - 2 * mine) * 128, 128), 128)],
            out_hbm.at[:, pl.ds(pl.multiple_of(s * 256, 256), 256)],
            load_sem.at[0],
        )

    def attend(t, carry):
        block = lax.rem(mine + 1 + t, blocks)
        at = pl.ds(pl.multiple_of(block * QB, QB), QB)
        for h in range(2):
            query = qaug[h, :, at]
            top = jnp.full((8, QB), -3e38, F32)
            for c in range(tokens // KB):
                rows = slice(c * KB, (c + 1) * KB)
                score = dot(kaug[h, rows, :], query)
                s_scr[h, rows, :] = score
                top = jnp.maximum(top, jnp.max(score.reshape(KB // 8, 8, QB), axis=0))
            top = jnp.max(top, axis=0, keepdims=True)
            for c in range(tokens // KB):
                rows = slice(c * KB, (c + 1) * KB)
                p_scr[h, rows, :] = jnp.exp2(s_scr[h, rows, :] - top).astype(BF)
            result = dot(vaug[h], p_scr[h])
            result = result[0:128, :] * (1.0 / result[128:129, :])
            ostage[block, :, h * 128 : (h + 1) * 128] = result.T.astype(BF)
        for side in range(2):

            @pl.when(2 * block + side != s)
            def _():
                o_copy(block, side, s).start()

            @pl.when(2 * block + side == s)
            def _():
                own_copy().start()

        return carry

    lax.fori_loop(0, blocks, attend, 0)

    @pl.when(e == 1)
    def _():
        for src in range(2):
            cache_copy(src, 0).wait_recv()
            forward_copy(src, core).start()
        for src in range(2):
            forward_copy(src, core).wait_send()
            forward_copy(src, 1 - core).wait_recv()

    @pl.when(e == 0)
    def _():
        for dst in range(4):
            z_copy(g, dst).wait_send()
        for dst in range(2):
            cache_copy(half, dst).wait_send()

    def x_done(k, carry):
        peer = lax.rem(s + k, n)
        x_copy(peer, s).wait_send()

        @pl.when(peer < red)
        def _():
            r_copy(peer, s).wait_send()

        @pl.when(s < red)
        def _():
            a_copy(peer, s).wait_send()

        o_copy(lax.div(peer, 2), lax.rem(peer, 2), s).wait_send()
        o_copy(0, 0, peer).wait_recv()
        return carry

    lax.fori_loop(1, n, x_done, 0)
    own_copy().wait()


def shards(
    n,
    latent,
    text_cache,
    patch_weight,
    patch_bias,
    qkv_weight,
    qk_gain,
    modulation,
    step_index,
    lengths,
    crossing,
):
    tokens = n * 128
    width = qkv_weight.shape[1]
    xt = latent[0, 0].T
    w3 = jnp.transpose(qkv_weight[0], (1, 0, 2))
    cache = text_cache[0, 0]
    smem = pl.BlockSpec(memory_space=pltpu.SMEM)
    vmem = pl.BlockSpec(memory_space=pltpu.VMEM)
    hbm = pl.BlockSpec(memory_space=pl.ANY)
    dma = pltpu.SemaphoreType.DMA
    red = ROWS // 8
    raw, land = pl.pallas_call(
        functools.partial(kernel, n),
        out_shape=(
            jax.ShapeDtypeStruct((128, n * 256), BF),
            jax.ShapeDtypeStruct((4,) + cache.shape, BF),
        ),
        in_specs=[smem] * 3 + [vmem] * 3 + [hbm] * 4,
        out_specs=(hbm, hbm),
        scratch_shapes=[
            pltpu.VMEM((64, width), BF),
            pltpu.VMEM(modulation.shape[1:], F32),
            pltpu.VMEM((3, width, 256), BF),
            pltpu.VMEM((2 * ROWS, width), BF),
            pltpu.VMEM((2 * ROWS, width), BF),
            pltpu.VMEM((4, 64, 128), BF),
            pltpu.VMEM((n, 64, 128), BF),
            pltpu.VMEM((3, 128, 256), F32),
            pltpu.VMEM((ROWS, 256), F32),
            pltpu.VMEM((n, 8, 256), F32),
            pltpu.VMEM((red, 8, 256), F32),
            pltpu.VMEM((256, tokens), BF),
            pltpu.VMEM((3, 256, 256), BF),
            pltpu.VMEM((3, 256, 128), F32),
            pltpu.VMEM((2, 256, tokens), BF),
            pltpu.VMEM((2, tokens, 256), BF),
            pltpu.VMEM((2, 144, tokens), BF),
            pltpu.VMEM((2, tokens, QB), F32),
            pltpu.VMEM((2, tokens, QB), BF),
            pltpu.VMEM((tokens // QB, QB, 256), BF),
            dma((5,)),
            dma((4,)),
            dma((4,)),
            dma((2,)),
            dma((2,)),
            dma((2,)),
            dma((2,)),
            dma((n,)),
            dma((n,)),
            dma((n,)),
            dma((n,)),
            dma((n,)),
            dma((n,)),
            dma((n,)),
            dma((n,)),
        ],
        compiler_params=pltpu.CompilerParams(
            collective_id=0, has_side_effects=True, vmem_limit_bytes=56 * 1024 * 1024
        ),
    )(
        crossing,
        lengths,
        step_index,
        xt,
        patch_bias,
        qk_gain[0],
        patch_weight[0],
        modulation[0],
        w3,
        cache,
    )

    expert_id = lax.axis_index("expert")
    group_id = lax.axis_index("group")
    seq_id = lax.axis_index("seq")
    dest_hit = crossing[:, 1] == group_id
    source_hit = crossing[:, 0] == group_id
    arrived = jnp.logical_and(expert_id == 1, jnp.any(dest_hit))
    vacated = jnp.logical_and(expert_id == 0, jnp.any(source_hit))
    source = jnp.sum(jnp.where(dest_hit, crossing[:, 0], 0))
    length = jnp.where(
        vacated, 0, jnp.where(arrived, lengths[0, source], lengths[expert_id, group_id])
    )
    row = seq_id * 128 + lax.broadcasted_iota(jnp.int32, raw.shape, 0)
    attended = jnp.where(row < length, raw, jnp.zeros_like(raw))
    moved = lax.dynamic_index_in_dim(land, source, 0, keepdims=False)
    cache_after = jnp.where(arrived, moved, jnp.where(vacated, jnp.zeros_like(cache), cache))
    return (attended[None, None], cache_after[None, None])


def solution(mesh):
    in_specs = (
        P("expert", "group", "seq", None),
        P("expert", "group", None, "seq", None),
        P("expert", None, None),
        P("expert", None),
        P("expert", None, None, "seq"),
        P("expert", None, "seq"),
        P("expert", None, None, None),
        P(),
        P(),
        P(),
    )
    out_specs = (P("expert", "group", "seq", None), P("expert", "group", None, "seq", None))
    return jax.shard_map(
        functools.partial(shards, mesh.shape["seq"]),
        mesh=mesh,
        in_specs=in_specs,
        out_specs=out_specs,
        check_vma=False,
    )
```

time: 352 us -> 63.8 us (0.18)
  the two profiles are of different devices: /device:TPU:32 before, /device:TPU:58 now
where the time goes in v1:
time: 63.8 us; the launch traced here: 63.5 us
  Pallas kernels  49.1 us (77%)
  other arithmetic  7.78 us (12%)
  between operations  5.16 us (8%)
  local copies, waits for them, and re-layouts  1.44 us (2%)
    pallas_call x1, Pallas kernels, shards(): pl.pallas_call(functools.partial(kernel, n), out_shape=(jax.ShapeDtypeStr...  49.1 us
    select_n x1, other arithmetic, shards(): jnp.where(arrived, moved, jnp.where(vacated, jnp.zeros_like(cache), cache))  2.44 us
    broadcast_in_dim x1, other arithmetic, shards(): return (attended[None, None], cache_after[None, None])  2.39 us
    reduce_or x1, other arithmetic, shards(): arrived = jnp.logical_and(expert_id == 1, jnp.any(dest_hit))  1.47 us
    reduce_sum x1, other arithmetic, shards(): source = jnp.sum(jnp.where(dest_hit, crossing[:, 0], 0))  1.46 us
    dynamic_slice x1, local copies, waits for them, and re-layouts, shards(): lengths[expert_id, group_id]  1.43 us

profile of v1, /device:TPU:58, one launch (start us, length us, event | category | flops | bytes accessed | tf_op | source)
XLA Modules:
  0.0 63.5 jit_solution(15672715523874144787)
XLA Ops:
  0.6 1.5 %select_reduce_fusion = s32[]{:T(128)} fusion(s32[2,2]{1,0:T(2,128)} %crossing.1, s32[]{:T(128)S(6)} %axis_index.38), kind=kLoop, calls=%fused_computation.4 | loop fusion | flops 5 | bytes 24 | tf_op jit(solution)/shard_map/reduce_sum | solution.py:562
  4.0 1.4 %fusion.1 = (s32[1,1]{1,0:T(1,128)}, s32[1,1]{1,0:T(1,128)}) fusion(s32[2,4]{1,0:T(2,128)} %lengths.1, s32[]{:T(128)S(6)} %select_n.46, s32[]{:T(128)S(6)} %select_n.47, s32[]{:T(128)S(6)} %select_n.45), kind=kLoop, calls=%fused_computation.9 | loop fusion | bytes 28 | tf_op jit(solution)/shard_map/dynamic_slice | solution.py:564
  5.5 1.5 %fusion = (pred[]{:T(512)}, pred[]{:T(512)}) fusion(s32[]{:T(128)S(6)} %axis_index.38, s32[2,2]{1,0:T(2,128)} %crossing.1), kind=kLoop, calls=%fused_computation.8 | loop fusion | flops 6 | bytes 22 | tf_op jit(solution)/shard_map/reduce_or | solution.py:560
  9.5 49.1 %shard_map.113 = (bf16[128,4096]{1,0:T(8,128)(2,1)}, bf16[4,512,2,256]{3,2,1,0:T(2,128)(2,1)}) custom-call(s32[2,2]{1,0:T(2,128)} %crossing.1, s32[2,4]{1,0:T(2,128)} %lengths.1, s32[2,4]{1,0:T(2,128)} %steps.1, bf16[64,128]{1,0:T(8,128)(2,1)} %bitcast.20, f32[1,5120]{1,0:T(1,128)} %b_ref.1, f32[2,256]{1,0:T(2,128)} %bitcast.21, bf16[64,5120]{1,0:T(8,128)(2,1)} %bitcast.19, ...), custom_call_target="tpu_custom_call" | custom-call | tf_op jit(solution)/shard_map/pallas_call | solution.py:494
  58.6 0.0 copy-start
  58.6 2.4 %select_bitcast_fusion = bf16[1,1,128,4096]{3,2,1,0:T(8,128)(2,1)} fusion(bf16[128,4096]{1,0:T(8,128)(2,1)} %get-tuple-element.4, pred[128]{0:T(512)(128)(4,1)S(1)} %add_compare_fusion), kind=kLoop, calls=%fused_computation | loop fusion | flops 524288 | bytes 2097280 | tf_op jit(solution)/shard_map/broadcast_in_dim | solution.py:570
  61.0 0.0 copy-done
  61.0 2.4 %broadcast_select_fusion.1 = bf16[1,1,512,2,256]{4,3,2,1,0:T(2,128)(2,1)} fusion(pred[]{:T(512)S(6)} %and.10, bf16[1,1,512,2,256]{4,3,2,1,0:T(2,128)(2,1)S(1)} %copy-done, pred[]{:T(512)S(6)} %and.9, bf16[4,512,2,256]{3,2,1,0:T(2,128)(2,1)} %get-tuple-element.5, s32[]{:T(128)S(6)} %select_n.45), kind=kLoop, calls=%fused_computation.2 | loop fusion | flops 524288 | bytes 1572870 | tf_op jit(solution)/shard_map/jit(_where)/select_n | solution.py:569
  (1 shorter events, 0.0 us)
Async XLA Ops:
  58.6 2.4 %copy-start = (bf16[1,1,512,2,256]{4,3,2,1,0:T(2,128)(2,1)S(1)}, bf16[1,1,512,2,256]{4,3,2,1,0:T(2,128)(2,1)}, u32[]{:S(2)}) copy-start(bf16[1,1,512,2,256]{4,3,2,1,0:T(2,128)(2,1)} %param.11) | copy-start | bytes 1572868

commit v2 on v1

v2 whole, which is shorter than its diff:
```python
import functools

import jax
import jax.numpy as jnp
from jax import lax
from jax.experimental import pallas as pl
from jax.experimental.pallas import tpu as pltpu
from jax.sharding import PartitionSpec as P

HD = 128
EPS = 1e-06
MASKED = -1e30
LOG2E = 1.4426950408889634
BF = jnp.bfloat16
F32 = jnp.float32
MESH = pl.DeviceIdType.MESH
ROWS = 80
RED = ROWS // 8
SIDE = 4
QB = 512
KB = 256
OWNERS = QB // 128
STEPS = (
    ((1, 0), (3, 0), (1, 2), (3, 2)),
    ((0, 1), (0, 3), (2, 1), (2, 3)),
    ((1, 1), (3, 3), (2, 0), (0, 2)),
    ((1, 3), (3, 1), (2, 2), (0, 0)),
)


def dot(a, b):
    return jnp.dot(a, b, preferred_element_type=F32)


def dot_nt(a, b):
    return lax.dot_general(a, b, (((1,), (1,)), ((), ())), preferred_element_type=F32)


def split(a):
    hi = a.astype(BF)
    lo = (a - hi.astype(F32)).astype(BF)
    return hi, lo


def gram(a):
    hi, lo = split(a)
    return dot_nt(hi, hi) + dot_nt(hi, lo) + dot_nt(lo, hi)


def pick(block, choices):
    value = choices[-1]
    for at in range(len(choices) - 2, -1, -1):
        value = jnp.where(block == at, choices[at], value)
    return value


def kernel(
    n,
    crossing,
    lengths,
    steps,
    xt_hbm,
    b_hbm,
    gain_hbm,
    p_hbm,
    mod_hbm,
    w_hbm,
    cache_hbm,
    out_hbm,
    land_hbm,
    x_v,
    b_v,
    gain_v,
    p_v,
    mod_v,
    w_v,
    a2,
    c2,
    zin,
    xall,
    m_v,
    gbuf,
    rs_in,
    ag,
    z2,
    mt2,
    mtf,
    qaug,
    kaug,
    vaug,
    s_a,
    s_b,
    ostage,
    load_sem,
    zsend,
    zrecv,
    csend,
    crecv,
    fsend,
    frecv,
    xsend,
    xrecv,
    rsend,
    rrecv,
    asend,
    arecv,
    osend,
    orecv,
):
    e = lax.axis_index("expert")
    g = lax.axis_index("group")
    s = lax.axis_index("seq")
    half = lax.div(g, 2)
    core = lax.rem(g, 2)
    my_x = lax.div(s, SIDE)
    my_y = lax.rem(s, SIDE)
    tokens = n * 128
    width = p_v.shape[1]

    def owner(step):
        return lax.rem(my_x + step[0], SIDE) * SIDE + lax.rem(my_y + step[1], SIDE)

    order = [owner(step) for block in STEPS for step in block]

    ld_p = pltpu.make_async_copy(p_hbm, p_v, load_sem.at[0])
    ld_b = pltpu.make_async_copy(b_hbm, b_v, load_sem.at[1])
    ld_x = pltpu.make_async_copy(xt_hbm, x_v, load_sem.at[2])
    ld_mod = pltpu.make_async_copy(mod_hbm, mod_v, load_sem.at[3])
    ld_gain = pltpu.make_async_copy(gain_hbm, gain_v, load_sem.at[4])
    ld_w = [pltpu.make_async_copy(w_hbm.at[j], w_v.at[j], load_sem.at[5 + j]) for j in range(3)]
    for copy in [ld_p, ld_b, ld_x, ld_mod, ld_gain] + ld_w:
        copy.start()

    barrier = pltpu.get_barrier_semaphore()

    def greet(k, carry):
        pl.semaphore_signal(barrier, inc=1, device_id={"seq": lax.rem(s + k, n)}, device_id_type=MESH)
        return carry

    for other in range(4):
        pl.semaphore_signal(
            barrier, inc=1, device_id={"expert": 1 - e, "group": other}, device_id_type=MESH
        )
    lax.fori_loop(1, n, greet, 0)

    @pl.when(e == 1)
    def _():
        pl.semaphore_signal(barrier, inc=1, device_id={"group": 2 * half + 1 - core}, device_id_type=MESH)

    hit0 = crossing[0, 1] == g
    hit1 = crossing[1, 1] == g
    arrived = jnp.logical_and(e == 1, jnp.logical_or(hit0, hit1))
    left = jnp.logical_and(e == 0, jnp.logical_or(crossing[0, 0] == g, crossing[1, 0] == g))
    source = jnp.where(hit0, crossing[0, 0], jnp.where(hit1, crossing[1, 0], 0))
    step_now = jnp.where(arrived, steps[0, source], steps[e, g])
    length = jnp.where(left, 0, jnp.where(arrived, lengths[0, source], lengths[e, g]))

    ld_p.wait()
    p_mean = jnp.mean(p_v[...].astype(F32), axis=1, keepdims=True)
    part = 1024
    for i in range(width // part):
        cols = pl.ds(i * part, part)
        hi, lo = split(p_v[:, cols].astype(F32) - p_mean)
        c2[0:64, cols] = hi
        c2[64:128, cols] = lo

    pl.semaphore_wait(barrier, n - 1 + 4 + e)

    def z_copy(src_group, dst_group):
        return pltpu.make_async_remote_copy(
            src_ref=xt_hbm,
            dst_ref=zin.at[src_group],
            send_sem=zsend.at[dst_group],
            recv_sem=zrecv.at[src_group],
            device_id={"expert": 1, "group": dst_group},
            device_id_type=MESH,
        )

    def cache_copy(src_half, dst_half):
        return pltpu.make_async_remote_copy(
            src_ref=cache_hbm,
            dst_ref=land_hbm.at[2 * src_half + core],
            send_sem=csend.at[dst_half],
            recv_sem=crecv.at[src_half],
            device_id={"expert": 1, "group": 2 * dst_half + core},
            device_id_type=MESH,
        )

    def forward_copy(src_half, src_core):
        return pltpu.make_async_remote_copy(
            src_ref=land_hbm.at[2 * src_half + src_core],
            dst_ref=land_hbm.at[2 * src_half + src_core],
            send_sem=fsend.at[src_half],
            recv_sem=frecv.at[src_half],
            device_id={"expert": 1, "group": 2 * half + 1 - core},
            device_id_type=MESH,
        )

    @pl.when(e == 0)
    def _():
        for dst in range(4):
            z_copy(g, dst).start()
        for dst in range(2):
            cache_copy(half, dst).start()

    ld_b.wait()
    ld_mod.wait()
    b_mean = jnp.mean(b_v[...], axis=1, keepdims=True)
    tail_row = lax.broadcasted_iota(jnp.int32, (16, part), 0)
    for i in range(width // part):
        cols = pl.ds(i * part, part)
        modulate = mod_v[step_now, :, cols]
        scale = 1.0 + modulate[1:2, :]
        shift = modulate[0:1, :]
        top = (p_v[:, cols].astype(F32) - p_mean) * scale
        bias = (b_v[:, cols] - b_mean) * scale
        bottom = jnp.where(
            tail_row == 0,
            jnp.broadcast_to(bias, (16, part)),
            jnp.where(tail_row == 1, jnp.broadcast_to(shift, (16, part)), 0.0),
        )
        hi, lo = split(top)
        a2[0:64, cols] = hi
        a2[ROWS : ROWS + 64, cols] = lo
        hi, lo = split(bottom)
        a2[64:ROWS, cols] = hi
        a2[ROWS + 64 : 2 * ROWS, cols] = lo

    def x_copy(peer, slot):
        return pltpu.make_async_remote_copy(
            src_ref=xall.at[slot],
            dst_ref=xall.at[slot],
            send_sem=xsend.at[peer],
            recv_sem=xrecv.at[slot],
            device_id={"seq": peer},
            device_id_type=MESH,
        )

    ld_x.wait()

    @pl.when(e == 1)
    def _():
        for src in range(4):
            z_copy(src, 0).wait_recv()
        xall[s] = jnp.where(arrived, zin[source], x_v[...])

    @pl.when(e == 0)
    def _():
        xall[s] = x_v[...]

    def x_start(k, carry):
        x_copy(lax.rem(s + k, n), s).start()
        return carry

    lax.fori_loop(1, n, x_start, 0)

    def project(j):
        raw = dot(a2[...], w_v[j])
        total = raw[0:ROWS, :] + raw[ROWS : 2 * ROWS, :]
        m_v[j, 0:ROWS, :] = total
        return total

    ld_w[0].wait()
    m_q = project(0)
    ld_w[1].wait()
    m_k = project(1)
    gbuf[...] = jnp.zeros_like(gbuf)
    gbuf[:, 0:ROWS] = gram(m_q)
    gbuf[:, 128 : 128 + ROWS] = gram(m_k)

    def r_copy(peer, slot):
        return pltpu.make_async_remote_copy(
            src_ref=gbuf.at[pl.ds(pl.multiple_of(peer * 8, 8), 8)],
            dst_ref=rs_in.at[slot],
            send_sem=rsend.at[peer],
            recv_sem=rrecv.at[slot],
            device_id={"seq": peer},
            device_id_type=MESH,
        )

    def r_start(k, carry):
        peer = lax.rem(s + k, n)

        @pl.when(peer < RED)
        def _():
            r_copy(peer, s).start()

        return carry

    lax.fori_loop(1, n, r_start, 0)

    own_t = xall[s].astype(F32).T.astype(BF)
    own_x = jnp.concatenate([own_t, own_t], axis=1)
    squares = jnp.zeros((128, 128), F32)
    for i in range(width // part):
        cols = pl.ds(i * part, part)
        centred = dot(own_x, c2[:, cols]) + (b_v[:, cols] - b_mean)
        centred = centred * centred
        for k in range(part // 128):
            squares = squares + centred[:, k * 128 : (k + 1) * 128]
    var = jnp.sum(squares, axis=1, keepdims=True) * (1.0 / width)
    own_rstd = jnp.broadcast_to(lax.rsqrt(var + EPS), (128, 128)).T

    ld_w[2].wait()
    project(2)

    def a_copy(peer, slot):
        return pltpu.make_async_remote_copy(
            src_ref=ag.at[slot],
            dst_ref=ag.at[slot],
            send_sem=asend.at[peer],
            recv_sem=arecv.at[slot],
            device_id={"seq": peer},
            device_id_type=MESH,
        )

    ag[s, :, 256:384] = own_rstd[0:8, :]

    @pl.when(s < RED)
    def _():
        def r_wait(k, carry):
            r_copy(0, lax.rem(s + k, n)).wait_recv()
            return carry

        lax.fori_loop(1, n, r_wait, 0)
        rs_in[s] = gbuf[pl.ds(pl.multiple_of(s * 8, 8), 8), :]
        total = rs_in[0]
        for src in range(1, n):
            total = total + rs_in[src]
        ag[s, :, 0:256] = total

    @pl.when(s >= RED)
    def _():
        ag[s, :, 0:256] = jnp.zeros((8, 256), F32)

    def a_start(k, carry):
        a_copy(lax.rem(s + k, n), s).start()
        return carry

    lax.fori_loop(1, n, a_start, 0)

    ld_gain.wait()
    for j in range(3):
        m_v[j, ROWS:128, :] = jnp.zeros((128 - ROWS, 256), F32)
        full = m_v[j]
        if j < 2:
            full = full * gain_v[j : j + 1, :]
        flipped = full.T
        hi, lo = split(flipped)
        mt2[j, :, 0:128] = hi
        mt2[j, :, 128:256] = lo
        mtf[j] = flipped

    first16 = lax.broadcasted_iota(jnp.int32, (16, tokens), 0)
    first128 = lax.broadcasted_iota(jnp.int32, (128, tokens), 0)
    one16 = jnp.where(first16 == 0, 1.0, 0.0).astype(BF)
    one128 = jnp.where(first128 == 0, 1.0, 0.0).astype(BF)
    for h in range(2):
        qaug[h, 128:256, :] = one128
        vaug[h, 128:144, :] = one16
    key_at = lax.broadcasted_iota(jnp.int32, (128, 128), 0)
    for i in range(n):
        masks = jnp.where(key_at + order[i] * 128 >= length, MASKED, 0.0).astype(BF)
        for h in range(2):
            kaug[h, i * 128 : (i + 1) * 128, 128:256] = masks

    def x_wait(k, carry):
        x_copy(0, lax.rem(s + k, n)).wait_recv()
        return carry

    lax.fori_loop(1, n, x_wait, 0)
    tail64 = lax.broadcasted_iota(jnp.int32, (64, 128), 0)
    ones_row = jnp.where(tail64 == 0, 1.0, 0.0).astype(BF)
    for i in range(n):
        cols = slice(i * 128, (i + 1) * 128)
        rows = xall[order[i]]
        z2[0:64, cols] = rows
        z2[128:192, cols] = rows
        z2[64:128, cols] = ones_row
        z2[192:256, cols] = ones_row

    def a_wait(k, carry):
        a_copy(0, lax.rem(s + k, n)).wait_recv()
        return carry

    lax.fori_loop(1, n, a_wait, 0)
    rstd = jnp.concatenate([ag[order[i], 0:1, 256:384] for i in range(n)], axis=1)
    both = jnp.concatenate([ag[d, :, 0:256] for d in range(RED)], axis=0)
    z0 = z2[0:128, :]
    z0f = z0[0:ROWS, :].astype(F32)
    scales = []
    for j in range(2):
        g_j = both[:, j * 128 : (j + 1) * 128]
        hi, lo = split(g_j)
        t = dot(hi, z0) + dot(lo, z0)
        quad = jnp.sum(t * z0f, axis=0, keepdims=True)
        total = rstd * rstd * quad + 2.0 * rstd * t[65:66, :] + g_j[65:66, 65:66]
        scales.append(lax.rsqrt(jnp.maximum(total, 0.0) * (1.0 / (n * 256)) + EPS))
    r_q = scales[0] * (LOG2E / HD**0.5)
    r_k = scales[1]

    piece = 512
    for i in range(tokens // piece):
        cols = slice(i * piece, (i + 1) * piece)
        rhs = z2[:, cols]
        r_i = rstd[:, cols]
        q_w = r_q[:, cols]
        k_w = r_k[:, cols]
        q_t = (dot(mt2[0], rhs) * (q_w * r_i) + mtf[0, :, 65:66] * q_w).astype(BF)
        k_t = dot(mt2[1], rhs) * (k_w * r_i) + mtf[1, :, 65:66] * k_w
        v_t = (dot(mt2[2], rhs) * r_i + mtf[2, :, 65:66]).astype(BF)
        for h in range(2):
            rows = slice(h * 128, (h + 1) * 128)
            qaug[h, 0:128, cols] = q_t[rows, :]
            vaug[h, 0:128, cols] = v_t[rows, :]
            kaug[h, cols, 0:128] = k_t[rows, :].T.astype(BF)

    blocks = tokens // QB

    def o_copy(block, side, h, peer, src):
        return pltpu.make_async_remote_copy(
            src_ref=ostage.at[h, block, pl.ds(side * 128, 128)],
            dst_ref=out_hbm.at[:, pl.ds(pl.multiple_of(src * 256 + h * 128, 128), 128)],
            send_sem=osend.at[h, OWNERS * block + side],
            recv_sem=orecv.at[h, src],
            device_id={"seq": peer},
            device_id_type=MESH,
        )

    def own_copy(h):
        return pltpu.make_async_copy(
            ostage.at[h, blocks - 1, pl.ds((OWNERS - 1) * 128, 128)],
            out_hbm.at[:, pl.ds(pl.multiple_of(s * 256 + h * 128, 128), 128)],
            load_sem.at[h],
        )

    def block_owner(block, side):
        return owner([pick(block, [STEPS[b][side][a] for b in range(blocks)]) for a in range(2)])

    def send(block, h):
        for side in range(OWNERS - 1):
            o_copy(block, side, h, block_owner(block, side), s).start()

        @pl.when(block < blocks - 1)
        def _():
            o_copy(block, OWNERS - 1, h, block_owner(block, OWNERS - 1), s).start()

        @pl.when(block == blocks - 1)
        def _():
            own_copy(h).start()

    def unit(block, h, now, top, next_block, next_h, later):
        query = qaug[next_h, :, pl.ds(pl.multiple_of(next_block * QB, QB), QB)]
        next_top = jnp.full((8, QB), -3e38, F32)
        total = jnp.zeros((144, QB), F32)
        for c in range(tokens // KB):
            rows = slice(c * KB, (c + 1) * KB)
            score = dot(kaug[next_h, rows, :], query)
            later[rows, :] = score
            next_top = jnp.maximum(next_top, jnp.max(score.reshape(KB // 8, 8, QB), axis=0))
            weight = jnp.exp2(now[rows, :] - top).astype(BF)
            total = total + dot(vaug[h, :, rows], weight)
        row = lax.broadcasted_iota(jnp.int32, (1, 128), 1)
        live = [row + block_owner(block, side) * 128 < length for side in range(OWNERS)]
        inverse = 1.0 / total[128:129, :]
        inverse = jnp.concatenate(
            [jnp.where(live[a], inverse[:, a * 128 : (a + 1) * 128], 0.0) for a in range(OWNERS)], axis=1
        )
        ostage[h, block] = (total[0:128, :] * inverse).T.astype(BF)
        return jnp.max(next_top, axis=0, keepdims=True)

    def attend(block, top):
        top = unit(block, 0, s_a, top, block, 1, s_b)
        send(block, 0)
        top = unit(block, 1, s_b, top, lax.rem(block + 1, blocks), 0, s_a)
        send(block, 1)
        return top

    first_top = jnp.full((8, QB), -3e38, F32)
    for c in range(tokens // KB):
        rows = slice(c * KB, (c + 1) * KB)
        score = dot(kaug[0, rows, :], qaug[0, :, 0:QB])
        s_a[rows, :] = score
        first_top = jnp.maximum(first_top, jnp.max(score.reshape(KB // 8, 8, QB), axis=0))
    lax.fori_loop(0, blocks, attend, jnp.max(first_top, axis=0, keepdims=True))

    @pl.when(e == 1)
    def _():
        for src in range(2):
            cache_copy(src, 0).wait_recv()
            forward_copy(src, core).start()
        for src in range(2):
            forward_copy(src, core).wait_send()
            forward_copy(src, 1 - core).wait_recv()

    @pl.when(e == 0)
    def _():
        for dst in range(4):
            z_copy(g, dst).wait_send()
        for dst in range(2):
            cache_copy(half, dst).wait_send()

    def finish(k, carry):
        peer = lax.rem(s + k, n)
        x_copy(peer, s).wait_send()
        a_copy(peer, s).wait_send()

        @pl.when(peer < RED)
        def _():
            r_copy(peer, s).wait_send()

        for h in range(2):
            o_copy(lax.div(k - 1, OWNERS), lax.rem(k - 1, OWNERS), h, peer, s).wait_send()
            o_copy(0, 0, h, peer, peer).wait_recv()
        return carry

    lax.fori_loop(1, n, finish, 0)
    for h in range(2):
        own_copy(h).wait()


def place(crossing, raw, land, cache, out, cache_out, rows_v, cache_v, sem):
    e = lax.axis_index("expert")
    g = lax.axis_index("group")
    hit0 = crossing[0, 1] == g
    hit1 = crossing[1, 1] == g
    arrived = jnp.logical_and(e == 1, jnp.logical_or(hit0, hit1))
    left = jnp.logical_and(e == 0, jnp.logical_or(crossing[0, 0] == g, crossing[1, 0] == g))
    source = jnp.where(hit0, crossing[0, 0], jnp.where(hit1, crossing[1, 0], 0))
    parts = 4
    height = raw.shape[0] // parts
    reads = []
    writes = []
    for i in range(parts):
        rows = pl.ds(i * height, height)
        reads.append(pltpu.make_async_copy(raw.at[rows], rows_v.at[rows], sem.at[0, i]))
        writes.append(pltpu.make_async_copy(rows_v.at[rows], out.at[rows], sem.at[1, i]))
    read_cache = pltpu.make_async_copy(cache, cache_v, sem.at[0, parts])
    write_cache = pltpu.make_async_copy(cache_v, cache_out, sem.at[1, parts])

    @pl.when(arrived)
    def _():
        pltpu.make_async_copy(land.at[source], cache_v, sem.at[0, parts]).start()

    @pl.when(jnp.logical_not(arrived))
    def _():
        read_cache.start()

    for copy in reads:
        copy.start()
    read_cache.wait()

    @pl.when(left)
    def _():
        cache_v[...] = jnp.zeros_like(cache_v)

    write_cache.start()
    for read, write in zip(reads, writes):
        read.wait()
        write.start()
    write_cache.wait()
    for write in writes:
        write.wait()


def shards(
    n,
    latent,
    text_cache,
    patch_weight,
    patch_bias,
    qkv_weight,
    qk_gain,
    modulation,
    step_index,
    lengths,
    crossing,
):
    tokens = n * 128
    width = qkv_weight.shape[1]
    xt = latent[0, 0].T
    w3 = jnp.transpose(qkv_weight[0], (1, 0, 2))
    cache = text_cache[0, 0]
    smem = pl.BlockSpec(memory_space=pltpu.SMEM)
    hbm = pl.BlockSpec(memory_space=pl.ANY)
    dma = pltpu.SemaphoreType.DMA
    raw, land = pl.pallas_call(
        functools.partial(kernel, n),
        out_shape=(
            jax.ShapeDtypeStruct((128, n * 256), BF),
            jax.ShapeDtypeStruct((4,) + cache.shape, BF),
        ),
        in_specs=[smem] * 3 + [hbm] * 7,
        out_specs=(hbm, hbm),
        scratch_shapes=[
            pltpu.VMEM((64, 128), BF),
            pltpu.VMEM((1, width), F32),
            pltpu.VMEM((2, 256), F32),
            pltpu.VMEM((64, width), BF),
            pltpu.VMEM(modulation.shape[1:], F32),
            pltpu.VMEM((3, width, 256), BF),
            pltpu.VMEM((2 * ROWS, width), BF),
            pltpu.VMEM((128, width), BF),
            pltpu.VMEM((4, 64, 128), BF),
            pltpu.VMEM((n, 64, 128), BF),
            pltpu.VMEM((3, 128, 256), F32),
            pltpu.VMEM((ROWS, 256), F32),
            pltpu.VMEM((n, 8, 256), F32),
            pltpu.VMEM((n, 8, 384), F32),
            pltpu.VMEM((256, tokens), BF),
            pltpu.VMEM((3, 256, 256), BF),
            pltpu.VMEM((3, 256, 128), F32),
            pltpu.VMEM((2, 256, tokens), BF),
            pltpu.VMEM((2, tokens, 256), BF),
            pltpu.VMEM((2, 144, tokens), BF),
            pltpu.VMEM((tokens, QB), F32),
            pltpu.VMEM((tokens, QB), F32),
            pltpu.VMEM((2, tokens // QB, QB, 128), BF),
            dma((8,)),
            dma((4,)),
            dma((4,)),
            dma((2,)),
            dma((2,)),
            dma((2,)),
            dma((2,)),
            dma((n,)),
            dma((n,)),
            dma((n,)),
            dma((n,)),
            dma((n,)),
            dma((n,)),
            dma((2, n)),
            dma((2, n)),
        ],
        compiler_params=pltpu.CompilerParams(
            collective_id=0, has_side_effects=True, vmem_limit_bytes=58 * 1024 * 1024
        ),
    )(
        crossing,
        lengths,
        step_index,
        xt,
        patch_bias,
        qk_gain[0],
        patch_weight[0],
        modulation[0],
        w3,
        cache,
    )
    attended, cache_after = pl.pallas_call(
        place,
        out_shape=(
            jax.ShapeDtypeStruct(raw.shape, BF),
            jax.ShapeDtypeStruct(cache.shape, BF),
        ),
        in_specs=[smem, hbm, hbm, hbm],
        out_specs=(hbm, hbm),
        scratch_shapes=[pltpu.VMEM(raw.shape, BF), pltpu.VMEM(cache.shape, BF), dma((2, 5))],
    )(crossing, raw, land, cache)
    return (attended[None, None], cache_after[None, None])


def solution(mesh):
    in_specs = (
        P("expert", "group", "seq", None),
        P("expert", "group", None, "seq", None),
        P("expert", None, None),
        P("expert", None),
        P("expert", None, None, "seq"),
        P("expert", None, "seq"),
        P("expert", None, None, None),
        P(),
        P(),
        P(),
    )
    out_specs = (P("expert", "group", "seq", None), P("expert", "group", None, "seq", None))
    return jax.shard_map(
        functools.partial(shards, mesh.shape["seq"]),
        mesh=mesh,
        in_specs=in_specs,
        out_specs=out_specs,
        check_vma=False,
    )
```

time: 63.8 us -> 48.4 us (0.76)
  the two profiles are of different devices: /device:TPU:58 before, /device:TPU:32 now
where the time goes in v2:
time: 48.4 us; the launch traced here: 48.3 us
  Pallas kernels  47.6 us (98%)
  between operations  0.64 us (1%)
    pallas_call x1, Pallas kernels, shards(): pl.pallas_call(functools.partial(kernel, n), out_shape=(jax.ShapeDtypeStr...  44.7 us
    pallas_call x1, Pallas kernels, shards(): pl.pallas_call(place, out_shape=(jax.ShapeDtypeStruct(raw.shape, BF), jax...  2.96 us

profile of v2, /device:TPU:32, one launch (start us, length us, event | category | flops | bytes accessed | tf_op | source)
XLA Modules:
  0.0 48.3 jit_solution(1502413337173495748)
XLA Ops:
  0.6 44.7 %shard_map.113 = (bf16[128,4096]{1,0:T(8,128)(2,1)}, bf16[4,512,2,256]{3,2,1,0:T(2,128)(2,1)}) custom-call(s32[2,2]{1,0:T(2,128)} %crossing.3, s32[2,4]{1,0:T(2,128)} %lengths.1, s32[2,4]{1,0:T(2,128)} %steps.1, bf16[64,128]{1,0:T(8,128)(2,1)} %bitcast.17, f32[1,5120]{1,0:T(1,128)} %b_hbm.1, f32[2,256]{1,0:T(2,128)} %bitcast.18, bf16[64,5120]{1,0:T(8,128)(2,1)} %bitcast.16, ...), custom_call_target="tpu_custom_call" | custom-call | tf_op jit(solution)/shard_map/pallas_call | solution.py:587
  45.3 3.0 %shard_map.114 = (bf16[128,4096]{1,0:T(8,128)(2,1)}, bf16[512,2,256]{2,1,0:T(2,128)(2,1)}) custom-call(s32[2,2]{1,0:T(2,128)} %crossing.3, bf16[128,4096]{1,0:T(8,128)(2,1)} %get-tuple-element.6.raw, bf16[4,512,2,256]{3,2,1,0:T(2,128)(2,1)} %get-tuple-element.7.land, bf16[512,2,256]{2,1,0:T(2,128)(2,1)} %bitcast.14), custom_call_target="tpu_custom_call" | custom-call | tf_op jit(solution)/shard_map/pallas_call | solution.py:650

commit v3 on v2

--- a/solution.py
+++ b/solution.py
@@ -15,7 +15,7 @@
 F32 = jnp.float32
 MESH = pl.DeviceIdType.MESH
 ROWS = 80
-RED = ROWS // 8
+PACKED = 40
 SIDE = 4
 QB = 512
 KB = 256
@@ -56,9 +56,9 @@
 
 def kernel(
     n,
-    crossing,
-    lengths,
-    steps,
+    crossing_hbm,
+    lengths_hbm,
+    steps_hbm,
     xt_hbm,
     b_hbm,
     gain_hbm,
@@ -68,6 +68,9 @@
     cache_hbm,
     out_hbm,
     land_hbm,
+    crossing,
+    lengths,
+    steps,
     x_v,
     b_v,
     gain_v,
@@ -80,11 +83,11 @@
     xall,
     m_v,
     gbuf,
-    rs_in,
-    ag,
+    g_in,
     z2,
     mt2,
     mtf,
+    raw_v,
     qaug,
     kaug,
     vaug,
@@ -100,10 +103,8 @@
     frecv,
     xsend,
     xrecv,
-    rsend,
-    rrecv,
-    asend,
-    arecv,
+    gsend,
+    grecv,
     osend,
     orecv,
 ):
@@ -128,7 +129,13 @@
     ld_mod = pltpu.make_async_copy(mod_hbm, mod_v, load_sem.at[3])
     ld_gain = pltpu.make_async_copy(gain_hbm, gain_v, load_sem.at[4])
     ld_w = [pltpu.make_async_copy(w_hbm.at[j], w_v.at[j], load_sem.at[5 + j]) for j in range(3)]
-    for copy in [ld_p, ld_b, ld_x, ld_mod, ld_gain] + ld_w:
+    ld_scalars = [
+        pltpu.make_async_copy(src, dst, load_sem.at[8 + i])
+        for i, (src, dst) in enumerate(
+            ((crossing_hbm, crossing), (lengths_hbm, lengths), (steps_hbm, steps))
+        )
+    ]
+    for copy in [ld_x] + ld_scalars + [ld_p, ld_b, ld_mod, ld_gain] + ld_w:
         copy.start()
 
     barrier = pltpu.get_barrier_semaphore()
@@ -146,25 +153,6 @@
     @pl.when(e == 1)
     def _():
         pl.semaphore_signal(barrier, inc=1, device_id={"group": 2 * half + 1 - core}, device_id_type=MESH)
-
-    hit0 = crossing[0, 1] == g
-    hit1 = crossing[1, 1] == g
-    arrived = jnp.logical_and(e == 1, jnp.logical_or(hit0, hit1))
-    left = jnp.logical_and(e == 0, jnp.logical_or(crossing[0, 0] == g, crossing[1, 0] == g))
-    source = jnp.where(hit0, crossing[0, 0], jnp.where(hit1, crossing[1, 0], 0))
-    step_now = jnp.where(arrived, steps[0, source], steps[e, g])
-    length = jnp.where(left, 0, jnp.where(arrived, lengths[0, source], lengths[e, g]))
-
-    ld_p.wait()
-    p_mean = jnp.mean(p_v[...].astype(F32), axis=1, keepdims=True)
-    part = 1024
-    for i in range(width // part):
-        cols = pl.ds(i * part, part)
-        hi, lo = split(p_v[:, cols].astype(F32) - p_mean)
-        c2[0:64, cols] = hi
-        c2[64:128, cols] = lo
-
-    pl.semaphore_wait(barrier, n - 1 + 4 + e)
 
     def z_copy(src_group, dst_group):
         return pltpu.make_async_remote_copy(
@@ -196,16 +184,48 @@
             device_id_type=MESH,
         )
 
+    def x_copy(peer, slot):
+        return pltpu.make_async_remote_copy(
+            src_ref=xall.at[slot],
+            dst_ref=xall.at[slot],
+            send_sem=xsend.at[peer],
+            recv_sem=xrecv.at[slot],
+            device_id={"seq": peer},
+            device_id_type=MESH,
+        )
+
+    def x_start(k, carry):
+        x_copy(lax.rem(s + k, n), s).start()
+        return carry
+
+    ld_x.wait()
+    pl.semaphore_wait(barrier, n - 1 + 4 + e)
+
     @pl.when(e == 0)
     def _():
         for dst in range(4):
             z_copy(g, dst).start()
+        xall[s] = x_v[...]
+        lax.fori_loop(1, n, x_start, 0)
         for dst in range(2):
             cache_copy(half, dst).start()
 
+    for copy in ld_scalars:
+        copy.wait()
+    hit0 = crossing[0, 1] == g
+    hit1 = crossing[1, 1] == g
+    arrived = jnp.logical_and(e == 1, jnp.logical_or(hit0, hit1))
+    left = jnp.logical_and(e == 0, jnp.logical_or(crossing[0, 0] == g, crossing[1, 0] == g))
+    source = jnp.where(hit0, crossing[0, 0], jnp.where(hit1, crossing[1, 0], 0))
+    step_now = jnp.where(arrived, steps[0, source], steps[e, g])
+    length = jnp.where(left, 0, jnp.where(arrived, lengths[0, source], lengths[e, g]))
+
+    ld_p.wait()
     ld_b.wait()
+    p_mean = jnp.mean(p_v[...].astype(F32), axis=1, keepdims=True)
+    b_mean = jnp.mean(b_v[...], axis=1, keepdims=True)
     ld_mod.wait()
-    b_mean = jnp.mean(b_v[...], axis=1, keepdims=True)
+    part = 1024
     tail_row = lax.broadcasted_iota(jnp.int32, (16, part), 0)
     for i in range(width // part):
         cols = pl.ds(i * part, part)
@@ -226,34 +246,6 @@
         a2[64:ROWS, cols] = hi
         a2[ROWS + 64 : 2 * ROWS, cols] = lo
 
-    def x_copy(peer, slot):
-        return pltpu.make_async_remote_copy(
-            src_ref=xall.at[slot],
-            dst_ref=xall.at[slot],
-            send_sem=xsend.at[peer],
-            recv_sem=xrecv.at[slot],
-            device_id={"seq": peer},
-            device_id_type=MESH,
-        )
-
-    ld_x.wait()
-
-    @pl.when(e == 1)
-    def _():
-        for src in range(4):
-            z_copy(src, 0).wait_recv()
-        xall[s] = jnp.where(arrived, zin[source], x_v[...])
-
-    @pl.when(e == 0)
-    def _():
-        xall[s] = x_v[...]
-
-    def x_start(k, carry):
-        x_copy(lax.rem(s + k, n), s).start()
-        return carry
-
-    lax.fori_loop(1, n, x_start, 0)
-
     def project(j):
         raw = dot(a2[...], w_v[j])
         total = raw[0:ROWS, :] + raw[ROWS : 2 * ROWS, :]
@@ -264,80 +256,63 @@
     m_q = project(0)
     ld_w[1].wait()
     m_k = project(1)
+
+    @pl.when(e == 1)
+    def _():
+        for src in range(4):
+            z_copy(src, 0).wait_recv()
+        xall[s] = jnp.where(arrived, zin[source], x_v[...])
+        lax.fori_loop(1, n, x_start, 0)
+
+    gram_q = gram(m_q)
+    gram_k = gram(m_k)
+    at_row = lax.broadcasted_iota(jnp.int32, (64, 64), 0)
+    at_col = lax.broadcasted_iota(jnp.int32, (64, 64), 1)
+    core_q = gram_q[0:64, 0:64]
+    core_k = gram_k[0:64, 0:64]
+    both = jnp.where(at_col < at_row, 2.0 * core_q, jnp.where(at_col == at_row, core_q, 2.0 * core_k))
     gbuf[...] = jnp.zeros_like(gbuf)
-    gbuf[:, 0:ROWS] = gram(m_q)
-    gbuf[:, 128 : 128 + ROWS] = gram(m_k)
-
-    def r_copy(peer, slot):
+    gbuf[0:32, 0:64] = both[0:32, :]
+    gbuf[0:32, 64:128] = both[32:64, :]
+    for at, values in enumerate((gram_q, gram_k)):
+        gbuf[32:34, at * 64 : at * 64 + 64] = values[64:66, 0:64]
+        gbuf[35 + 2 * at : 37 + 2 * at, 0:16] = values[64:66, 64:80]
+    gbuf[34:35, 0:64] = jnp.sum(jnp.where(at_col == at_row, core_k, 0.0), axis=0, keepdims=True)
+
+    def g_copy(peer, slot):
         return pltpu.make_async_remote_copy(
-            src_ref=gbuf.at[pl.ds(pl.multiple_of(peer * 8, 8), 8)],
-            dst_ref=rs_in.at[slot],
-            send_sem=rsend.at[peer],
-            recv_sem=rrecv.at[slot],
+            src_ref=gbuf,
+            dst_ref=g_in.at[slot],
+            send_sem=gsend.at[peer],
+            recv_sem=grecv.at[slot],
             device_id={"seq": peer},
             device_id_type=MESH,
         )
 
-    def r_start(k, carry):
-        peer = lax.rem(s + k, n)
-
-        @pl.when(peer < RED)
-        def _():
-            r_copy(peer, s).start()
-
+    def g_start(k, carry):
+        g_copy(lax.rem(s + k, n), s).start()
         return carry
 
-    lax.fori_loop(1, n, r_start, 0)
-
-    own_t = xall[s].astype(F32).T.astype(BF)
-    own_x = jnp.concatenate([own_t, own_t], axis=1)
-    squares = jnp.zeros((128, 128), F32)
+    lax.fori_loop(1, n, g_start, 0)
+    g_in[s] = gbuf[...]
+
     for i in range(width // part):
         cols = pl.ds(i * part, part)
-        centred = dot(own_x, c2[:, cols]) + (b_v[:, cols] - b_mean)
-        centred = centred * centred
-        for k in range(part // 128):
-            squares = squares + centred[:, k * 128 : (k + 1) * 128]
-    var = jnp.sum(squares, axis=1, keepdims=True) * (1.0 / width)
-    own_rstd = jnp.broadcast_to(lax.rsqrt(var + EPS), (128, 128)).T
+        hi, lo = split(p_v[:, cols].astype(F32) - p_mean)
+        c2[0:64, cols] = hi
+        c2[ROWS : ROWS + 64, cols] = lo
+        bias = jnp.broadcast_to(b_v[:, cols] - b_mean, (16, part))
+        hi, lo = split(jnp.where(tail_row == 0, bias, 0.0))
+        c2[64:ROWS, cols] = hi
+        c2[ROWS + 64 : 2 * ROWS, cols] = lo
+    var_gram = (
+        dot_nt(c2[0:ROWS, :], c2[0:ROWS, :])
+        + dot_nt(c2[0:ROWS, :], c2[ROWS : 2 * ROWS, :])
+        + dot_nt(c2[ROWS : 2 * ROWS, :], c2[0:ROWS, :])
+    ) * (1.0 / width)
 
     ld_w[2].wait()
     project(2)
-
-    def a_copy(peer, slot):
-        return pltpu.make_async_remote_copy(
-            src_ref=ag.at[slot],
-            dst_ref=ag.at[slot],
-            send_sem=asend.at[peer],
-            recv_sem=arecv.at[slot],
-            device_id={"seq": peer},
-            device_id_type=MESH,
-        )
-
-    ag[s, :, 256:384] = own_rstd[0:8, :]
-
-    @pl.when(s < RED)
-    def _():
-        def r_wait(k, carry):
-            r_copy(0, lax.rem(s + k, n)).wait_recv()
-            return carry
-
-        lax.fori_loop(1, n, r_wait, 0)
-        rs_in[s] = gbuf[pl.ds(pl.multiple_of(s * 8, 8), 8), :]
-        total = rs_in[0]
-        for src in range(1, n):
-            total = total + rs_in[src]
-        ag[s, :, 0:256] = total
-
-    @pl.when(s >= RED)
-    def _():
-        ag[s, :, 0:256] = jnp.zeros((8, 256), F32)
-
-    def a_start(k, carry):
-        a_copy(lax.rem(s + k, n), s).start()
-        return carry
-
-    lax.fori_loop(1, n, a_start, 0)
 
     ld_gain.wait()
     for j in range(3):
@@ -379,41 +354,66 @@
         z2[64:128, cols] = ones_row
         z2[192:256, cols] = ones_row
 
-    def a_wait(k, carry):
-        a_copy(0, lax.rem(s + k, n)).wait_recv()
-        return carry
-
-    lax.fori_loop(1, n, a_wait, 0)
-    rstd = jnp.concatenate([ag[order[i], 0:1, 256:384] for i in range(n)], axis=1)
-    both = jnp.concatenate([ag[d, :, 0:256] for d in range(RED)], axis=0)
-    z0 = z2[0:128, :]
-    z0f = z0[0:ROWS, :].astype(F32)
-    scales = []
-    for j in range(2):
-        g_j = both[:, j * 128 : (j + 1) * 128]
-        hi, lo = split(g_j)
-        t = dot(hi, z0) + dot(lo, z0)
-        quad = jnp.sum(t * z0f, axis=0, keepdims=True)
-        total = rstd * rstd * quad + 2.0 * rstd * t[65:66, :] + g_j[65:66, 65:66]
-        scales.append(lax.rsqrt(jnp.maximum(total, 0.0) * (1.0 / (n * 256)) + EPS))
-    r_q = scales[0] * (LOG2E / HD**0.5)
-    r_k = scales[1]
+    x64 = z2[0:64, :]
+    z80 = z2[0:ROWS, :]
+    hi, lo = split(var_gram)
+    t = dot(hi, z80) + dot(lo, z80)
+    var = jnp.maximum(jnp.sum(t * z80.astype(F32), axis=0, keepdims=True), 0.0)
+    rstd = lax.rsqrt(var + EPS)
 
     piece = 512
     for i in range(tokens // piece):
         cols = slice(i * piece, (i + 1) * piece)
         rhs = z2[:, cols]
         r_i = rstd[:, cols]
-        q_w = r_q[:, cols]
-        k_w = r_k[:, cols]
-        q_t = (dot(mt2[0], rhs) * (q_w * r_i) + mtf[0, :, 65:66] * q_w).astype(BF)
-        k_t = dot(mt2[1], rhs) * (k_w * r_i) + mtf[1, :, 65:66] * k_w
+        for j in range(2):
+            raw_v[j, :, cols] = dot(mt2[j], rhs) * r_i + mtf[j, :, 65:66]
         v_t = (dot(mt2[2], rhs) * r_i + mtf[2, :, 65:66]).astype(BF)
         for h in range(2):
+            vaug[h, 0:128, cols] = v_t[h * 128 : (h + 1) * 128, :]
+
+    def g_wait(k, carry):
+        g_copy(0, lax.rem(s + k, n)).wait_recv()
+        return carry
+
+    lax.fori_loop(1, n, g_wait, 0)
+    packed = g_in[0]
+    for src in range(1, n):
+        packed = packed + g_in[src]
+    both = jnp.concatenate([packed[0:32, 0:64], packed[0:32, 64:128]], axis=0)
+    lower = jnp.where(at_col <= at_row, both, 0.0)
+    diagonal = jnp.where(at_col == at_row, jnp.broadcast_to(packed[34:35, 0:64], (64, 64)), 0.0)
+    upper = jnp.where(at_col > at_row, both, diagonal)
+    tail16 = lax.broadcasted_iota(jnp.int32, (16, 64), 0)
+    linear = jnp.zeros((16, 64), F32)
+    for at, row in enumerate(
+        (packed[32:33, 0:64], packed[33:34, 0:64], packed[32:33, 64:128], packed[33:34, 64:128])
+    ):
+        linear = jnp.where(tail16 == at, jnp.broadcast_to(row, (16, 64)), linear)
+    hi, lo = split(jnp.concatenate([lower, upper, linear], axis=0))
+    t = dot(hi, x64) + dot(lo, x64)
+    xf = x64.astype(F32)
+    scales = []
+    for j in range(2):
+        quad = jnp.sum(t[j * 64 : j * 64 + 64, :] * xf, axis=0, keepdims=True)
+        by_bias = t[128 + 2 * j : 129 + 2 * j, :]
+        by_shift = t[129 + 2 * j : 130 + 2 * j, :]
+        at = 35 + 2 * j
+        total = (
+            rstd * rstd * (quad + 2.0 * by_bias + packed[at : at + 1, 0:1])
+            + 2.0 * rstd * (by_shift + packed[at : at + 1, 1:2])
+            + packed[at + 1 : at + 2, 1:2]
+        )
+        scales.append(lax.rsqrt(jnp.maximum(total, 0.0) * (1.0 / (n * 256)) + EPS))
+    r_q = scales[0] * (LOG2E / HD**0.5)
+    r_k = scales[1]
+
+    for i in range(tokens // piece):
+        cols = slice(i * piece, (i + 1) * piece)
+        for h in range(2):
             rows = slice(h * 128, (h + 1) * 128)
-            qaug[h, 0:128, cols] = q_t[rows, :]
-            vaug[h, 0:128, cols] = v_t[rows, :]
-            kaug[h, cols, 0:128] = k_t[rows, :].T.astype(BF)
+            qaug[h, 0:128, cols] = (raw_v[0, rows, cols] * r_q[:, cols]).astype(BF)
+            kaug[h, cols, 0:128] = (raw_v[1, rows, cols] * r_k[:, cols]).T.astype(BF)
 
     blocks = tokens // QB
 
@@ -474,6 +474,13 @@
         send(block, 0)
         top = unit(block, 1, s_b, top, lax.rem(block + 1, blocks), 0, s_a)
         send(block, 1)
+
+        @pl.when(jnp.logical_and(e == 1, block == blocks // 2))
+        def _():
+            for src in range(2):
+                cache_copy(src, 0).wait_recv()
+                forward_copy(src, core).start()
+
         return top
 
     first_top = jnp.full((8, QB), -3e38, F32)
@@ -487,9 +494,6 @@
     @pl.when(e == 1)
     def _():
         for src in range(2):
-            cache_copy(src, 0).wait_recv()
-            forward_copy(src, core).start()
-        for src in range(2):
             forward_copy(src, core).wait_send()
             forward_copy(src, 1 - core).wait_recv()
 
@@ -503,12 +507,7 @@
     def finish(k, carry):
         peer = lax.rem(s + k, n)
         x_copy(peer, s).wait_send()
-        a_copy(peer, s).wait_send()
-
-        @pl.when(peer < RED)
-        def _():
-            r_copy(peer, s).wait_send()
-
+        g_copy(peer, s).wait_send()
         for h in range(2):
             o_copy(lax.div(k - 1, OWNERS), lax.rem(k - 1, OWNERS), h, peer, s).wait_send()
             o_copy(0, 0, h, peer, peer).wait_recv()
@@ -519,14 +518,11 @@
         own_copy(h).wait()
 
 
-def place(crossing, raw, land, cache, out, cache_out, rows_v, cache_v, sem):
+def place(crossing_hbm, raw, land, cache, out, cache_out, crossing, rows_v, cache_v, sem):
     e = lax.axis_index("expert")
     g = lax.axis_index("group")
-    hit0 = crossing[0, 1] == g
-    hit1 = crossing[1, 1] == g
-    arrived = jnp.logical_and(e == 1, jnp.logical_or(hit0, hit1))
-    left = jnp.logical_and(e == 0, jnp.logical_or(crossing[0, 0] == g, crossing[1, 0] == g))
-    source = jnp.where(hit0, crossing[0, 0], jnp.where(hit1, crossing[1, 0], 0))
+    scalars = pltpu.make_async_copy(crossing_hbm, crossing, sem.at[0, 5])
+    scalars.start()
     parts = 4
     height = raw.shape[0] // parts
     reads = []
@@ -535,9 +531,18 @@
         rows = pl.ds(i * height, height)
         reads.append(pltpu.make_async_copy(raw.at[rows], rows_v.at[rows], sem.at[0, i]))
         writes.append(pltpu.make_async_copy(rows_v.at[rows], out.at[rows], sem.at[1, i]))
+    for copy in reads:
+        copy.start()
     read_cache = pltpu.make_async_copy(cache, cache_v, sem.at[0, parts])
     write_cache = pltpu.make_async_copy(cache_v, cache_out, sem.at[1, parts])
 
+    scalars.wait()
+    hit0 = crossing[0, 1] == g
+    hit1 = crossing[1, 1] == g
+    arrived = jnp.logical_and(e == 1, jnp.logical_or(hit0, hit1))
+    left = jnp.logical_and(e == 0, jnp.logical_or(crossing[0, 0] == g, crossing[1, 0] == g))
+    source = jnp.where(hit0, crossing[0, 0], jnp.where(hit1, crossing[1, 0], 0))
+
     @pl.when(arrived)
     def _():
         pltpu.make_async_copy(land.at[source], cache_v, sem.at[0, parts]).start()
@@ -546,8 +551,6 @@
     def _():
         read_cache.start()
 
-    for copy in reads:
-        copy.start()
     read_cache.wait()
 
     @pl.when(left)
@@ -581,7 +584,6 @@
     xt = latent[0, 0].T
     w3 = jnp.transpose(qkv_weight[0], (1, 0, 2))
     cache = text_cache[0, 0]
-    smem = pl.BlockSpec(memory_space=pltpu.SMEM)
     hbm = pl.BlockSpec(memory_space=pl.ANY)
     dma = pltpu.SemaphoreType.DMA
     raw, land = pl.pallas_call(
@@ -590,9 +592,12 @@
             jax.ShapeDtypeStruct((128, n * 256), BF),
             jax.ShapeDtypeStruct((4,) + cache.shape, BF),
         ),
-        in_specs=[smem] * 3 + [hbm] * 7,
+        in_specs=[hbm] * 10,
         out_specs=(hbm, hbm),
         scratch_shapes=[
+            pltpu.SMEM((2, 2), jnp.int32),
+            pltpu.SMEM((2, 4), jnp.int32),
+            pltpu.SMEM((2, 4), jnp.int32),
             pltpu.VMEM((64, 128), BF),
             pltpu.VMEM((1, width), F32),
             pltpu.VMEM((2, 256), F32),
@@ -600,31 +605,29 @@
             pltpu.VMEM(modulation.shape[1:], F32),
             pltpu.VMEM((3, width, 256), BF),
             pltpu.VMEM((2 * ROWS, width), BF),
-            pltpu.VMEM((128, width), BF),
+            pltpu.VMEM((2 * ROWS, width), BF),
             pltpu.VMEM((4, 64, 128), BF),
             pltpu.VMEM((n, 64, 128), BF),
             pltpu.VMEM((3, 128, 256), F32),
-            pltpu.VMEM((ROWS, 256), F32),
-            pltpu.VMEM((n, 8, 256), F32),
-            pltpu.VMEM((n, 8, 384), F32),
+            pltpu.VMEM((PACKED, 128), F32),
+            pltpu.VMEM((n, PACKED, 128), F32),
             pltpu.VMEM((256, tokens), BF),
             pltpu.VMEM((3, 256, 256), BF),
             pltpu.VMEM((3, 256, 128), F32),
+            pltpu.VMEM((2, 256, tokens), F32),
             pltpu.VMEM((2, 256, tokens), BF),
             pltpu.VMEM((2, tokens, 256), BF),
             pltpu.VMEM((2, 144, tokens), BF),
             pltpu.VMEM((tokens, QB), F32),
             pltpu.VMEM((tokens, QB), F32),
             pltpu.VMEM((2, tokens // QB, QB, 128), BF),
-            dma((8,)),
+            dma((11,)),
             dma((4,)),
             dma((4,)),
             dma((2,)),
             dma((2,)),
             dma((2,)),
             dma((2,)),
-            dma((n,)),
-            dma((n,)),
             dma((n,)),
             dma((n,)),
             dma((n,)),
@@ -653,9 +656,14 @@
             jax.ShapeDtypeStruct(raw.shape, BF),
             jax.ShapeDtypeStruct(cache.shape, BF),
         ),
-        in_specs=[smem, hbm, hbm, hbm],
+        in_specs=[hbm] * 4,
         out_specs=(hbm, hbm),
-        scratch_shapes=[pltpu.VMEM(raw.shape, BF), pltpu.VMEM(cache.shape, BF), dma((2, 5))],
+        scratch_shapes=[
+            pltpu.SMEM((2, 2), jnp.int32),
+            pltpu.VMEM(raw.shape, BF),
+            pltpu.VMEM(cache.shape, BF),
+            dma((2, 6)),
+        ],
     )(crossing, raw, land, cache)
     return (attended[None, None], cache_after[None, None])
 

time: 48.4 us -> 43.5 us (0.90)
  Pallas kernels: 47.6 us -> 42.7 us
    pallas_call x1, Pallas kernels: 44.7 us -> 39.6 us  [shards(): pl.pallas_call(functools.partial(kernel, n), out_shape=(jax.ShapeDtypeStr...]
where the time goes in v3:
time: 43.5 us; the launch traced here: 43.3 us
  Pallas kernels  42.7 us (98%)
  between operations  0.64 us (1%)
    pallas_call x1, Pallas kernels, shards(): pl.pallas_call(functools.partial(kernel, n), out_shape=(jax.ShapeDtypeStr...  39.6 us
    pallas_call x1, Pallas kernels, shards(): pl.pallas_call(place, out_shape=(jax.ShapeDtypeStruct(raw.shape, BF), jax...  3.05 us

profile of v3, /device:TPU:32, one launch (start us, length us, event | category | flops | bytes accessed | tf_op | source)
XLA Modules:
  0.0 43.3 jit_solution(1888828206986309755)
XLA Ops:
  0.6 39.6 %shard_map.113 = (bf16[128,4096]{1,0:T(8,128)(2,1)}, bf16[4,512,2,256]{3,2,1,0:T(2,128)(2,1)}) custom-call(s32[2,2]{1,0:T(2,128)} %crossing_hbm.3, s32[2,4]{1,0:T(2,128)} %lengths_hbm.1, s32[2,4]{1,0:T(2,128)} %steps_hbm.1, bf16[64,128]{1,0:T(8,128)(2,1)} %bitcast.17, f32[1,5120]{1,0:T(1,128)} %b_hbm.1, f32[2,256]{1,0:T(2,128)} %bitcast.18, ...), custom_call_target="tpu_custom_call" | custom-call | tf_op jit(solution)/shard_map/pallas_call | solution.py:589
  40.3 3.1 %shard_map.114 = (bf16[128,4096]{1,0:T(8,128)(2,1)}, bf16[512,2,256]{2,1,0:T(2,128)(2,1)}) custom-call(s32[2,2]{1,0:T(2,128)} %crossing_hbm.3, bf16[128,4096]{1,0:T(8,128)(2,1)} %get-tuple-element.6.raw, bf16[4,512,2,256]{3,2,1,0:T(2,128)(2,1)} %get-tuple-element.7.land, bf16[512,2,256]{2,1,0:T(2,128)(2,1)} %bitcast.14), custom_call_target="tpu_custom_call" | custom-call | tf_op jit(solution)/shard_map/pallas_call | solution.py:653

commit v4 on v3

--- a/solution.py
+++ b/solution.py
@@ -21,10 +21,10 @@
 KB = 256
 OWNERS = QB // 128
 STEPS = (
-    ((1, 0), (3, 0), (1, 2), (3, 2)),
-    ((0, 1), (0, 3), (2, 1), (2, 3)),
-    ((1, 1), (3, 3), (2, 0), (0, 2)),
-    ((1, 3), (3, 1), (2, 2), (0, 0)),
+    ((1, 0), (3, 0), (1, 2), (3, 2))
+    + ((0, 1), (0, 3), (2, 1), (2, 3))
+    + ((1, 1), (3, 3), (2, 0), (0, 2))
+    + ((1, 3), (3, 1), (2, 2), (0, 0))
 )
 
 
@@ -67,7 +67,7 @@
     w_hbm,
     cache_hbm,
     out_hbm,
-    land_hbm,
+    cache_out,
     crossing,
     lengths,
     steps,
@@ -87,13 +87,14 @@
     z2,
     mt2,
     mtf,
-    raw_v,
     qaug,
     kaug,
     vaug,
     s_a,
     s_b,
     ostage,
+    own_cache,
+    land,
     load_sem,
     zsend,
     zrecv,
@@ -121,7 +122,7 @@
     def owner(step):
         return lax.rem(my_x + step[0], SIDE) * SIDE + lax.rem(my_y + step[1], SIDE)
 
-    order = [owner(step) for block in STEPS for step in block]
+    order = [owner(step) for step in STEPS]
 
     ld_p = pltpu.make_async_copy(p_hbm, p_v, load_sem.at[0])
     ld_b = pltpu.make_async_copy(b_hbm, b_v, load_sem.at[1])
@@ -135,7 +136,9 @@
             ((crossing_hbm, crossing), (lengths_hbm, lengths), (steps_hbm, steps))
         )
     ]
-    for copy in [ld_x] + ld_scalars + [ld_p, ld_b, ld_mod, ld_gain] + ld_w:
+    ld_cache = pltpu.make_async_copy(cache_hbm, own_cache, load_sem.at[11])
+    st_cache = pltpu.make_async_copy(own_cache, cache_out, load_sem.at[11])
+    for copy in [ld_x] + ld_scalars + [ld_p, ld_b, ld_mod, ld_gain] + ld_w + [ld_cache]:
         copy.start()
 
     barrier = pltpu.get_barrier_semaphore()
@@ -167,7 +170,7 @@
     def cache_copy(src_half, dst_half):
         return pltpu.make_async_remote_copy(
             src_ref=cache_hbm,
-            dst_ref=land_hbm.at[2 * src_half + core],
+            dst_ref=land.at[2 * src_half + core],
             send_sem=csend.at[dst_half],
             recv_sem=crecv.at[src_half],
             device_id={"expert": 1, "group": 2 * dst_half + core},
@@ -176,8 +179,8 @@
 
     def forward_copy(src_half, src_core):
         return pltpu.make_async_remote_copy(
-            src_ref=land_hbm.at[2 * src_half + src_core],
-            dst_ref=land_hbm.at[2 * src_half + src_core],
+            src_ref=land.at[2 * src_half + src_core],
+            dst_ref=land.at[2 * src_half + src_core],
             send_sem=fsend.at[src_half],
             recv_sem=frecv.at[src_half],
             device_id={"expert": 1, "group": 2 * half + 1 - core},
@@ -188,9 +191,19 @@
         return pltpu.make_async_remote_copy(
             src_ref=xall.at[slot],
             dst_ref=xall.at[slot],
-            send_sem=xsend.at[peer],
-            recv_sem=xrecv.at[slot],
+            send_sem=xsend,
+            recv_sem=xrecv,
             device_id={"seq": peer},
+            device_id_type=MESH,
+        )
+
+    def x_all():
+        return pltpu.make_async_remote_copy(
+            src_ref=xall.at[pl.ds(0, n - 1)],
+            dst_ref=xall.at[pl.ds(0, n - 1)],
+            send_sem=xsend,
+            recv_sem=xrecv,
+            device_id={"seq": lax.rem(s + 1, n)},
             device_id_type=MESH,
         )
 
@@ -257,13 +270,6 @@
     ld_w[1].wait()
     m_k = project(1)
 
-    @pl.when(e == 1)
-    def _():
-        for src in range(4):
-            z_copy(src, 0).wait_recv()
-        xall[s] = jnp.where(arrived, zin[source], x_v[...])
-        lax.fori_loop(1, n, x_start, 0)
-
     gram_q = gram(m_q)
     gram_k = gram(m_k)
     at_row = lax.broadcasted_iota(jnp.int32, (64, 64), 0)
@@ -283,9 +289,19 @@
         return pltpu.make_async_remote_copy(
             src_ref=gbuf,
             dst_ref=g_in.at[slot],
-            send_sem=gsend.at[peer],
-            recv_sem=grecv.at[slot],
+            send_sem=gsend,
+            recv_sem=grecv,
             device_id={"seq": peer},
+            device_id_type=MESH,
+        )
+
+    def g_all():
+        return pltpu.make_async_remote_copy(
+            src_ref=g_in.at[pl.ds(0, n - 1)],
+            dst_ref=g_in.at[pl.ds(0, n - 1)],
+            send_sem=gsend,
+            recv_sem=grecv,
+            device_id={"seq": lax.rem(s + 1, n)},
             device_id_type=MESH,
         )
 
@@ -294,6 +310,14 @@
         return carry
 
     lax.fori_loop(1, n, g_start, 0)
+
+    @pl.when(e == 1)
+    def _():
+        for src in range(4):
+            z_copy(src, 0).wait_recv()
+        xall[s] = jnp.where(arrived, zin[source], x_v[...])
+        lax.fori_loop(1, n, x_start, 0)
+
     g_in[s] = gbuf[...]
 
     for i in range(width // part):
@@ -322,8 +346,8 @@
             full = full * gain_v[j : j + 1, :]
         flipped = full.T
         hi, lo = split(flipped)
-        mt2[j, :, 0:128] = hi
-        mt2[j, :, 128:256] = lo
+        mt2[j * 256 : (j + 1) * 256, 0:128] = hi
+        mt2[j * 256 : (j + 1) * 256, 128:256] = lo
         mtf[j] = flipped
 
     first16 = lax.broadcasted_iota(jnp.int32, (16, tokens), 0)
@@ -339,11 +363,7 @@
         for h in range(2):
             kaug[h, i * 128 : (i + 1) * 128, 128:256] = masks
 
-    def x_wait(k, carry):
-        x_copy(0, lax.rem(s + k, n)).wait_recv()
-        return carry
-
-    lax.fori_loop(1, n, x_wait, 0)
+    x_all().wait_recv()
     tail64 = lax.broadcasted_iota(jnp.int32, (64, 128), 0)
     ones_row = jnp.where(tail64 == 0, 1.0, 0.0).astype(BF)
     for i in range(n):
@@ -364,19 +384,11 @@
     piece = 512
     for i in range(tokens // piece):
         cols = slice(i * piece, (i + 1) * piece)
-        rhs = z2[:, cols]
-        r_i = rstd[:, cols]
-        for j in range(2):
-            raw_v[j, :, cols] = dot(mt2[j], rhs) * r_i + mtf[j, :, 65:66]
-        v_t = (dot(mt2[2], rhs) * r_i + mtf[2, :, 65:66]).astype(BF)
+        v_t = (dot(mt2[512:768, :], z2[:, cols]) * rstd[:, cols] + mtf[2, :, 65:66]).astype(BF)
         for h in range(2):
             vaug[h, 0:128, cols] = v_t[h * 128 : (h + 1) * 128, :]
 
-    def g_wait(k, carry):
-        g_copy(0, lax.rem(s + k, n)).wait_recv()
-        return carry
-
-    lax.fori_loop(1, n, g_wait, 0)
+    g_all().wait_recv()
     packed = g_in[0]
     for src in range(1, n):
         packed = packed + g_in[src]
@@ -408,12 +420,17 @@
     r_q = scales[0] * (LOG2E / HD**0.5)
     r_k = scales[1]
 
+    q_u = r_q * rstd
+    k_u = r_k * rstd
     for i in range(tokens // piece):
         cols = slice(i * piece, (i + 1) * piece)
+        raw = dot(mt2[0:512, :], z2[:, cols])
+        q_t = (raw[0:256, :] * q_u[:, cols] + mtf[0, :, 65:66] * r_q[:, cols]).astype(BF)
+        k_t = raw[256:512, :] * k_u[:, cols] + mtf[1, :, 65:66] * r_k[:, cols]
         for h in range(2):
             rows = slice(h * 128, (h + 1) * 128)
-            qaug[h, 0:128, cols] = (raw_v[0, rows, cols] * r_q[:, cols]).astype(BF)
-            kaug[h, cols, 0:128] = (raw_v[1, rows, cols] * r_k[:, cols]).T.astype(BF)
+            qaug[h, 0:128, cols] = q_t[rows, :]
+            kaug[h, cols, 0:128] = k_t[rows, :].T.astype(BF)
 
     blocks = tokens // QB
 
@@ -421,9 +438,19 @@
         return pltpu.make_async_remote_copy(
             src_ref=ostage.at[h, block, pl.ds(side * 128, 128)],
             dst_ref=out_hbm.at[:, pl.ds(pl.multiple_of(src * 256 + h * 128, 128), 128)],
-            send_sem=osend.at[h, OWNERS * block + side],
-            recv_sem=orecv.at[h, src],
+            send_sem=osend,
+            recv_sem=orecv,
             device_id={"seq": peer},
+            device_id_type=MESH,
+        )
+
+    def o_all():
+        return pltpu.make_async_remote_copy(
+            src_ref=out_hbm.at[:, pl.ds(0, (n - 1) * 256)],
+            dst_ref=out_hbm.at[:, pl.ds(0, (n - 1) * 256)],
+            send_sem=osend,
+            recv_sem=orecv,
+            device_id={"seq": lax.rem(s + 1, n)},
             device_id_type=MESH,
         )
 
@@ -435,7 +462,7 @@
         )
 
     def block_owner(block, side):
-        return owner([pick(block, [STEPS[b][side][a] for b in range(blocks)]) for a in range(2)])
+        return owner([pick(block, [STEPS[b * OWNERS + side][a] for b in range(blocks)]) for a in range(2)])
 
     def send(block, h):
         for side in range(OWNERS - 1):
@@ -491,11 +518,21 @@
         first_top = jnp.maximum(first_top, jnp.max(score.reshape(KB // 8, 8, QB), axis=0))
     lax.fori_loop(0, blocks, attend, jnp.max(first_top, axis=0, keepdims=True))
 
+    ld_cache.wait()
+    height = own_cache.shape[0] // 8
+
     @pl.when(e == 1)
     def _():
         for src in range(2):
             forward_copy(src, core).wait_send()
             forward_copy(src, 1 - core).wait_recv()
+
+        def choose(i, carry):
+            rows = pl.ds(i * height, height)
+            own_cache[rows] = jnp.where(arrived, land[source, rows], own_cache[rows])
+            return carry
+
+        lax.fori_loop(0, 8, choose, 0)
 
     @pl.when(e == 0)
     def _():
@@ -504,66 +541,41 @@
         for dst in range(2):
             cache_copy(half, dst).wait_send()
 
-    def finish(k, carry):
-        peer = lax.rem(s + k, n)
-        x_copy(peer, s).wait_send()
-        g_copy(peer, s).wait_send()
-        for h in range(2):
-            o_copy(lax.div(k - 1, OWNERS), lax.rem(k - 1, OWNERS), h, peer, s).wait_send()
-            o_copy(0, 0, h, peer, peer).wait_recv()
-        return carry
-
-    lax.fori_loop(1, n, finish, 0)
+        def choose(i, carry):
+            rows = pl.ds(i * height, height)
+            kept = own_cache[rows]
+            own_cache[rows] = jnp.where(left, jnp.zeros_like(kept), kept)
+            return carry
+
+        lax.fori_loop(0, 8, choose, 0)
+
+    st_cache.start()
+    x_all().wait_send()
+    g_all().wait_send()
+    o_all().wait_send()
     for h in range(2):
         own_copy(h).wait()
-
-
-def place(crossing_hbm, raw, land, cache, out, cache_out, crossing, rows_v, cache_v, sem):
-    e = lax.axis_index("expert")
-    g = lax.axis_index("group")
-    scalars = pltpu.make_async_copy(crossing_hbm, crossing, sem.at[0, 5])
-    scalars.start()
+    st_cache.wait()
+    o_all().wait_recv()
+
+
+def place(raw, cache, out, cache_out, rows_v, cache_v, sem):
     parts = 4
-    height = raw.shape[0] // parts
     reads = []
     writes = []
-    for i in range(parts):
-        rows = pl.ds(i * height, height)
-        reads.append(pltpu.make_async_copy(raw.at[rows], rows_v.at[rows], sem.at[0, i]))
-        writes.append(pltpu.make_async_copy(rows_v.at[rows], out.at[rows], sem.at[1, i]))
+    for at, (src, mid, dst) in enumerate(((raw, rows_v, out), (cache, cache_v, cache_out))):
+        height = src.shape[0] // parts
+        for i in range(parts):
+            rows = pl.ds(i * height, height)
+            reads.append(pltpu.make_async_copy(src.at[rows], mid.at[rows], sem.at[0, at, i]))
+            writes.append(pltpu.make_async_copy(mid.at[rows], dst.at[rows], sem.at[1, at, i]))
     for copy in reads:
         copy.start()
-    read_cache = pltpu.make_async_copy(cache, cache_v, sem.at[0, parts])
-    write_cache = pltpu.make_async_copy(cache_v, cache_out, sem.at[1, parts])
-
-    scalars.wait()
-    hit0 = crossing[0, 1] == g
-    hit1 = crossing[1, 1] == g
-    arrived = jnp.logical_and(e == 1, jnp.logical_or(hit0, hit1))
-    left = jnp.logical_and(e == 0, jnp.logical_or(crossing[0, 0] == g, crossing[1, 0] == g))
-    source = jnp.where(hit0, crossing[0, 0], jnp.where(hit1, crossing[1, 0], 0))
-
-    @pl.when(arrived)
-    def _():
-        pltpu.make_async_copy(land.at[source], cache_v, sem.at[0, parts]).start()
-
-    @pl.when(jnp.logical_not(arrived))
-    def _():
-        read_cache.start()
-
-    read_cache.wait()
-
-    @pl.when(left)
-    def _():
-        cache_v[...] = jnp.zeros_like(cache_v)
-
-    write_cache.start()
     for read, write in zip(reads, writes):
         read.wait()
         write.start()
-    write_cache.wait()
-    for write in writes:
-        write.wait()
+    for copy in writes:
+        copy.wait()
 
 
 def shards(
@@ -586,11 +598,11 @@
     cache = text_cache[0, 0]
     hbm = pl.BlockSpec(memory_space=pl.ANY)
     dma = pltpu.SemaphoreType.DMA
-    raw, land = pl.pallas_call(
+    raw, chosen = pl.pallas_call(
         functools.partial(kernel, n),
         out_shape=(
             jax.ShapeDtypeStruct((128, n * 256), BF),
-            jax.ShapeDtypeStruct((4,) + cache.shape, BF),
+            jax.ShapeDtypeStruct(cache.shape, BF),
         ),
         in_specs=[hbm] * 10,
         out_specs=(hbm, hbm),
@@ -612,28 +624,29 @@
             pltpu.VMEM((PACKED, 128), F32),
             pltpu.VMEM((n, PACKED, 128), F32),
             pltpu.VMEM((256, tokens), BF),
-            pltpu.VMEM((3, 256, 256), BF),
+            pltpu.VMEM((768, 256), BF),
             pltpu.VMEM((3, 256, 128), F32),
-            pltpu.VMEM((2, 256, tokens), F32),
             pltpu.VMEM((2, 256, tokens), BF),
             pltpu.VMEM((2, tokens, 256), BF),
             pltpu.VMEM((2, 144, tokens), BF),
             pltpu.VMEM((tokens, QB), F32),
             pltpu.VMEM((tokens, QB), F32),
             pltpu.VMEM((2, tokens // QB, QB, 128), BF),
-            dma((11,)),
+            pltpu.VMEM(cache.shape, BF),
+            pltpu.VMEM((4,) + cache.shape, BF),
+            dma((12,)),
             dma((4,)),
             dma((4,)),
             dma((2,)),
             dma((2,)),
             dma((2,)),
             dma((2,)),
-            dma((n,)),
-            dma((n,)),
-            dma((n,)),
-            dma((n,)),
-            dma((2, n)),
-            dma((2, n)),
+            dma,
+            dma,
+            dma,
+            dma,
+            dma,
+            dma,
         ],
         compiler_params=pltpu.CompilerParams(
             collective_id=0, has_side_effects=True, vmem_limit_bytes=58 * 1024 * 1024
@@ -656,15 +669,14 @@
             jax.ShapeDtypeStruct(raw.shape, BF),
             jax.ShapeDtypeStruct(cache.shape, BF),
         ),
-        in_specs=[hbm] * 4,
+        in_specs=[hbm] * 2,
         out_specs=(hbm, hbm),
         scratch_shapes=[
-            pltpu.SMEM((2, 2), jnp.int32),
             pltpu.VMEM(raw.shape, BF),
             pltpu.VMEM(cache.shape, BF),
-            dma((2, 6)),
+            dma((2, 2, 4)),
         ],
-    )(crossing, raw, land, cache)
+    )(raw, chosen)
     return (attended[None, None], cache_after[None, None])
 
 

time: 43.5 us -> 40 us (0.920)
  Pallas kernels: 42.7 us -> 39.2 us
    pallas_call x1, Pallas kernels: 39.6 us -> 37 us  [shards(): pl.pallas_call(functools.partial(kernel, n), out_shape=(jax.ShapeDtypeStr...]
    pallas_call x1, Pallas kernels: 3.05 us -> 2.22 us  [shards(): pl.pallas_call(place, out_shape=(jax.ShapeDtypeStruct(raw.shape, BF), jax...]
where the time goes in v4:
time: 40 us; the launch traced here: 39.9 us
  Pallas kernels  39.2 us (98%)
  between operations  0.64 us (2%)
    pallas_call x1, Pallas kernels, shards(): pl.pallas_call(functools.partial(kernel, n), out_shape=(jax.ShapeDtypeStr...  37 us
    pallas_call x1, Pallas kernels, shards(): pl.pallas_call(place, out_shape=(jax.ShapeDtypeStruct(raw.shape, BF), jax...  2.22 us

profile of v4, /device:TPU:32, one launch (start us, length us, event | category | flops | bytes accessed | tf_op | source)
XLA Modules:
  0.0 39.9 jit_solution(1025319908757848591)
XLA Ops:
  0.6 37.0 %shard_map.113 = (bf16[128,4096]{1,0:T(8,128)(2,1)}, bf16[512,2,256]{2,1,0:T(2,128)(2,1)}) custom-call(s32[2,2]{1,0:T(2,128)} %crossing_hbm.1, s32[2,4]{1,0:T(2,128)} %lengths_hbm.1, s32[2,4]{1,0:T(2,128)} %steps_hbm.1, bf16[64,128]{1,0:T(8,128)(2,1)} %bitcast.16, f32[1,5120]{1,0:T(1,128)} %b_hbm.1, f32[2,256]{1,0:T(2,128)} %bitcast.17, ...), custom_call_target="tpu_custom_call" | custom-call | tf_op jit(solution)/shard_map/pallas_call | solution.py:601
  37.7 2.2 %shard_map.114 = (bf16[128,4096]{1,0:T(8,128)(2,1)}, bf16[512,2,256]{2,1,0:T(2,128)(2,1)}) custom-call(bf16[128,4096]{1,0:T(8,128)(2,1)} %get-tuple-element.6.raw, bf16[512,2,256]{2,1,0:T(2,128)(2,1)} %get-tuple-element.7.cache), custom_call_target="tpu_custom_call" | custom-call | tf_op jit(solution)/shard_map/pallas_call | solution.py:666

commit v5 on v4

--- a/solution.py
+++ b/solution.py
@@ -21,10 +21,10 @@
 KB = 256
 OWNERS = QB // 128
 STEPS = (
-    ((1, 0), (3, 0), (1, 2), (3, 2))
-    + ((0, 1), (0, 3), (2, 1), (2, 3))
-    + ((1, 1), (3, 3), (2, 0), (0, 2))
-    + ((1, 3), (3, 1), (2, 2), (0, 0))
+    ((2, 2), (1, 1), (3, 3), (2, 0))
+    + ((0, 2), (1, 2), (3, 1), (2, 3))
+    + ((1, 3), (3, 2), (2, 1), (0, 3))
+    + ((1, 0), (3, 0), (0, 1), (0, 0))
 )
 
 
@@ -45,13 +45,6 @@
 def gram(a):
     hi, lo = split(a)
     return dot_nt(hi, hi) + dot_nt(hi, lo) + dot_nt(lo, hi)
-
-
-def pick(block, choices):
-    value = choices[-1]
-    for at in range(len(choices) - 2, -1, -1):
-        value = jnp.where(block == at, choices[at], value)
-    return value
 
 
 def kernel(
@@ -84,6 +77,7 @@
     m_v,
     gbuf,
     g_in,
+    stat,
     z2,
     mt2,
     mtf,
@@ -138,7 +132,7 @@
     ]
     ld_cache = pltpu.make_async_copy(cache_hbm, own_cache, load_sem.at[11])
     st_cache = pltpu.make_async_copy(own_cache, cache_out, load_sem.at[11])
-    for copy in [ld_x] + ld_scalars + [ld_p, ld_b, ld_mod, ld_gain] + ld_w + [ld_cache]:
+    for copy in [ld_x] + ld_scalars + [ld_p, ld_b, ld_mod, ld_gain, ld_w[0], ld_w[1]]:
         copy.start()
 
     barrier = pltpu.get_barrier_semaphore()
@@ -159,7 +153,7 @@
 
     def z_copy(src_group, dst_group):
         return pltpu.make_async_remote_copy(
-            src_ref=xt_hbm,
+            src_ref=x_v,
             dst_ref=zin.at[src_group],
             send_sem=zsend.at[dst_group],
             recv_sem=zrecv.at[src_group],
@@ -266,6 +260,8 @@
         return total
 
     ld_w[0].wait()
+    ld_w[2].start()
+    ld_cache.start()
     m_q = project(0)
     ld_w[1].wait()
     m_k = project(1)
@@ -346,8 +342,11 @@
             full = full * gain_v[j : j + 1, :]
         flipped = full.T
         hi, lo = split(flipped)
-        mt2[j * 256 : (j + 1) * 256, 0:128] = hi
-        mt2[j * 256 : (j + 1) * 256, 128:256] = lo
+        for h in range(2):
+            at = 512 + h * 128 if j == 2 else h * 256 + j * 128
+            rows = slice(h * 128, (h + 1) * 128)
+            mt2[at : at + 128, 0:128] = hi[rows, :]
+            mt2[at : at + 128, 128:256] = lo[rows, :]
         mtf[j] = flipped
 
     first16 = lax.broadcasted_iota(jnp.int32, (16, tokens), 0)
@@ -363,31 +362,14 @@
         for h in range(2):
             kaug[h, i * 128 : (i + 1) * 128, 128:256] = masks
 
-    x_all().wait_recv()
-    tail64 = lax.broadcasted_iota(jnp.int32, (64, 128), 0)
+    tail64 = lax.broadcasted_iota(jnp.int32, (64, tokens), 0)
     ones_row = jnp.where(tail64 == 0, 1.0, 0.0).astype(BF)
-    for i in range(n):
-        cols = slice(i * 128, (i + 1) * 128)
-        rows = xall[order[i]]
-        z2[0:64, cols] = rows
-        z2[128:192, cols] = rows
-        z2[64:128, cols] = ones_row
-        z2[192:256, cols] = ones_row
-
-    x64 = z2[0:64, :]
-    z80 = z2[0:ROWS, :]
+    z2[64:128, :] = ones_row
+    z2[192:256, :] = ones_row
     hi, lo = split(var_gram)
-    t = dot(hi, z80) + dot(lo, z80)
-    var = jnp.maximum(jnp.sum(t * z80.astype(F32), axis=0, keepdims=True), 0.0)
-    rstd = lax.rsqrt(var + EPS)
-
-    piece = 512
-    for i in range(tokens // piece):
-        cols = slice(i * piece, (i + 1) * piece)
-        v_t = (dot(mt2[512:768, :], z2[:, cols]) * rstd[:, cols] + mtf[2, :, 65:66]).astype(BF)
-        for h in range(2):
-            vaug[h, 0:128, cols] = v_t[h * 128 : (h + 1) * 128, :]
-
+    stat[...] = jnp.zeros_like(stat)
+    stat[0:ROWS, 0:ROWS] = hi
+    stat[0:ROWS, 128 : 128 + ROWS] = lo
     g_all().wait_recv()
     packed = g_in[0]
     for src in range(1, n):
@@ -403,13 +385,26 @@
     ):
         linear = jnp.where(tail16 == at, jnp.broadcast_to(row, (16, 64)), linear)
     hi, lo = split(jnp.concatenate([lower, upper, linear], axis=0))
-    t = dot(hi, x64) + dot(lo, x64)
-    xf = x64.astype(F32)
+    stat[ROWS : ROWS + 144, 0:64] = hi
+    stat[ROWS : ROWS + 144, 128:192] = lo
+
+    x_all().wait_recv()
+    for i in range(n):
+        cols = slice(i * 128, (i + 1) * 128)
+        rows = xall[order[i]]
+        z2[0:64, cols] = rows
+        z2[128:192, cols] = rows
+    t = dot(stat[...], z2[...])
+    z80 = z2[0:ROWS, :].astype(F32)
+    var = jnp.maximum(jnp.sum(t[0:ROWS, :] * z80, axis=0, keepdims=True), 0.0)
+    rstd = lax.rsqrt(var + EPS)
     scales = []
     for j in range(2):
-        quad = jnp.sum(t[j * 64 : j * 64 + 64, :] * xf, axis=0, keepdims=True)
-        by_bias = t[128 + 2 * j : 129 + 2 * j, :]
-        by_shift = t[129 + 2 * j : 130 + 2 * j, :]
+        base = ROWS + j * 64
+        quad = jnp.sum(t[base : base + 64, :] * z80[0:64, :], axis=0, keepdims=True)
+        base = ROWS + 128 + 2 * j
+        by_bias = t[base : base + 1, :]
+        by_shift = t[base + 1 : base + 2, :]
         at = 35 + 2 * j
         total = (
             rstd * rstd * (quad + 2.0 * by_bias + packed[at : at + 1, 0:1])
@@ -422,101 +417,117 @@
 
     q_u = r_q * rstd
     k_u = r_k * rstd
-    for i in range(tokens // piece):
-        cols = slice(i * piece, (i + 1) * piece)
-        raw = dot(mt2[0:512, :], z2[:, cols])
-        q_t = (raw[0:256, :] * q_u[:, cols] + mtf[0, :, 65:66] * r_q[:, cols]).astype(BF)
-        k_t = raw[256:512, :] * k_u[:, cols] + mtf[1, :, 65:66] * r_k[:, cols]
-        for h in range(2):
+    piece = 512
+
+    def heads(h):
+        for i in range(tokens // piece):
+            cols = slice(i * piece, (i + 1) * piece)
+            raw = dot(mt2[h * 256 : (h + 1) * 256, :], z2[:, cols])
             rows = slice(h * 128, (h + 1) * 128)
-            qaug[h, 0:128, cols] = q_t[rows, :]
-            kaug[h, cols, 0:128] = k_t[rows, :].T.astype(BF)
-
-    blocks = tokens // QB
-
-    def o_copy(block, side, h, peer, src):
-        return pltpu.make_async_remote_copy(
-            src_ref=ostage.at[h, block, pl.ds(side * 128, 128)],
-            dst_ref=out_hbm.at[:, pl.ds(pl.multiple_of(src * 256 + h * 128, 128), 128)],
-            send_sem=osend,
-            recv_sem=orecv,
-            device_id={"seq": peer},
-            device_id_type=MESH,
-        )
-
-    def o_all():
-        return pltpu.make_async_remote_copy(
-            src_ref=out_hbm.at[:, pl.ds(0, (n - 1) * 256)],
-            dst_ref=out_hbm.at[:, pl.ds(0, (n - 1) * 256)],
-            send_sem=osend,
-            recv_sem=orecv,
-            device_id={"seq": lax.rem(s + 1, n)},
-            device_id_type=MESH,
-        )
-
-    def own_copy(h):
-        return pltpu.make_async_copy(
-            ostage.at[h, blocks - 1, pl.ds((OWNERS - 1) * 128, 128)],
-            out_hbm.at[:, pl.ds(pl.multiple_of(s * 256 + h * 128, 128), 128)],
-            load_sem.at[h],
-        )
-
-    def block_owner(block, side):
-        return owner([pick(block, [STEPS[b * OWNERS + side][a] for b in range(blocks)]) for a in range(2)])
-
-    def send(block, h):
-        for side in range(OWNERS - 1):
-            o_copy(block, side, h, block_owner(block, side), s).start()
-
-        @pl.when(block < blocks - 1)
-        def _():
-            o_copy(block, OWNERS - 1, h, block_owner(block, OWNERS - 1), s).start()
-
-        @pl.when(block == blocks - 1)
-        def _():
-            own_copy(h).start()
-
-    def unit(block, h, now, top, next_block, next_h, later):
-        query = qaug[next_h, :, pl.ds(pl.multiple_of(next_block * QB, QB), QB)]
-        next_top = jnp.full((8, QB), -3e38, F32)
-        total = jnp.zeros((144, QB), F32)
-        for c in range(tokens // KB):
-            rows = slice(c * KB, (c + 1) * KB)
-            score = dot(kaug[next_h, rows, :], query)
-            later[rows, :] = score
-            next_top = jnp.maximum(next_top, jnp.max(score.reshape(KB // 8, 8, QB), axis=0))
-            weight = jnp.exp2(now[rows, :] - top).astype(BF)
-            total = total + dot(vaug[h, :, rows], weight)
-        row = lax.broadcasted_iota(jnp.int32, (1, 128), 1)
-        live = [row + block_owner(block, side) * 128 < length for side in range(OWNERS)]
-        inverse = 1.0 / total[128:129, :]
-        inverse = jnp.concatenate(
-            [jnp.where(live[a], inverse[:, a * 128 : (a + 1) * 128], 0.0) for a in range(OWNERS)], axis=1
-        )
-        ostage[h, block] = (total[0:128, :] * inverse).T.astype(BF)
-        return jnp.max(next_top, axis=0, keepdims=True)
-
-    def attend(block, top):
-        top = unit(block, 0, s_a, top, block, 1, s_b)
-        send(block, 0)
-        top = unit(block, 1, s_b, top, lax.rem(block + 1, blocks), 0, s_a)
-        send(block, 1)
-
-        @pl.when(jnp.logical_and(e == 1, block == blocks // 2))
-        def _():
-            for src in range(2):
-                cache_copy(src, 0).wait_recv()
-                forward_copy(src, core).start()
-
-        return top
-
+            qaug[h, 0:128, cols] = (
+                raw[0:128, :] * q_u[:, cols] + mtf[0, rows, 65:66] * r_q[:, cols]
+            ).astype(BF)
+            k_t = raw[128:256, :] * k_u[:, cols] + mtf[1, rows, 65:66] * r_k[:, cols]
+            kaug[h, cols, 0:128] = k_t.T.astype(BF)
+
+    heads(0)
     first_top = jnp.full((8, QB), -3e38, F32)
     for c in range(tokens // KB):
         rows = slice(c * KB, (c + 1) * KB)
         score = dot(kaug[0, rows, :], qaug[0, :, 0:QB])
         s_a[rows, :] = score
         first_top = jnp.maximum(first_top, jnp.max(score.reshape(KB // 8, 8, QB), axis=0))
-    lax.fori_loop(0, blocks, attend, jnp.max(first_top, axis=0, keepdims=True))
+    def values(h):
+        for i in range(tokens // piece):
+            cols = slice(i * piece, (i + 1) * piece)
+            rows = slice(h * 128, (h + 1) * 128)
+            raw = dot(mt2[512 + h * 128 : 640 + h * 128, :], z2[:, cols])
+            vaug[h, 0:128, cols] = (raw * rstd[:, cols] + mtf[2, rows, 65:66]).astype(BF)
+
+    blocks = tokens // QB
+
+    def o_copy(block, side, h, peer, src):
+        return pltpu.make_async_remote_copy(
+            src_ref=ostage.at[h, block, pl.ds(side * 128, 128)],
+            dst_ref=out_hbm.at[:, pl.ds(pl.multiple_of(src * 256 + h * 128, 128), 128)],
+            send_sem=osend,
+            recv_sem=orecv,
+            device_id={"seq": peer},
+            device_id_type=MESH,
+        )
+
+    def o_all():
+        return pltpu.make_async_remote_copy(
+            src_ref=out_hbm.at[:, pl.ds(0, (n - 1) * 256)],
+            dst_ref=out_hbm.at[:, pl.ds(0, (n - 1) * 256)],
+            send_sem=osend,
+            recv_sem=orecv,
+            device_id={"seq": lax.rem(s + 1, n)},
+            device_id_type=MESH,
+        )
+
+    def own_copy(h):
+        return pltpu.make_async_copy(
+            ostage.at[h, blocks - 1, pl.ds((OWNERS - 1) * 128, 128)],
+            out_hbm.at[:, pl.ds(pl.multiple_of(s * 256 + h * 128, 128), 128)],
+            load_sem.at[h],
+        )
+
+    def send(block, h):
+        for side in range(OWNERS - 1):
+            o_copy(block, side, h, order[block * OWNERS + side], s).start()
+
+        if block == blocks - 1:
+            own_copy(h).start()
+        else:
+            o_copy(block, OWNERS - 1, h, order[block * OWNERS + OWNERS - 1], s).start()
+
+    def unit(block, h, now, top, next_block, next_h, later):
+        ahead = later is not None
+        if ahead:
+            query = qaug[next_h, :, next_block * QB : (next_block + 1) * QB]
+        next_top = jnp.full((8, QB), -3e38, F32)
+        total = jnp.zeros((144, QB), F32)
+        for c in range(tokens // KB):
+            rows = slice(c * KB, (c + 1) * KB)
+            if ahead:
+                score = dot(kaug[next_h, rows, :], query)
+                later[rows, :] = score
+                next_top = jnp.maximum(next_top, jnp.max(score.reshape(KB // 8, 8, QB), axis=0))
+            weight = jnp.exp2(now[rows, :] - top).astype(BF)
+            total = total + dot(vaug[h, :, rows], weight)
+        row = lax.broadcasted_iota(jnp.int32, (1, 128), 1)
+        live = [row + order[block * OWNERS + side] * 128 < length for side in range(OWNERS)]
+        inverse = 1.0 / total[128:129, :]
+        inverse = jnp.concatenate(
+            [jnp.where(live[a], inverse[:, a * 128 : (a + 1) * 128], 0.0) for a in range(OWNERS)], axis=1
+        )
+        ostage[h, block] = (total[0:128, :] * inverse).T.astype(BF)
+        return jnp.max(next_top, axis=0, keepdims=True)
+
+    def forward():
+        @pl.when(e == 1)
+        def _():
+            for src in range(2):
+                cache_copy(src, 0).wait_recv()
+                forward_copy(src, core).start()
+
+    units = [(block, h) for h in range(2) for block in range(blocks)]
+    halves = (s_a, s_b)
+    values(0)
+    top = jnp.max(first_top, axis=0, keepdims=True)
+    for at, (block, h) in enumerate(units):
+        if at == 2:
+            heads(1)
+        if at == blocks:
+            values(1)
+        if at == len(units) - 2:
+            forward()
+        if at + 1 < len(units):
+            top = unit(block, h, halves[at % 2], top, *units[at + 1], halves[(at + 1) % 2])
+        else:
+            unit(block, h, halves[at % 2], top, None, None, None)
+        send(block, h)
 
     ld_cache.wait()
     height = own_cache.shape[0] // 8
@@ -559,21 +570,16 @@
     o_all().wait_recv()
 
 
-def place(raw, cache, out, cache_out, rows_v, cache_v, sem):
+def place(raw, cache, out, cache_out, sem):
     parts = 4
-    reads = []
     writes = []
-    for at, (src, mid, dst) in enumerate(((raw, rows_v, out), (cache, cache_v, cache_out))):
+    for at, (src, dst) in enumerate(((raw, out), (cache, cache_out))):
         height = src.shape[0] // parts
         for i in range(parts):
             rows = pl.ds(i * height, height)
-            reads.append(pltpu.make_async_copy(src.at[rows], mid.at[rows], sem.at[0, at, i]))
-            writes.append(pltpu.make_async_copy(mid.at[rows], dst.at[rows], sem.at[1, at, i]))
-    for copy in reads:
+            writes.append(pltpu.make_async_copy(src.at[rows], dst.at[rows], sem.at[at, i]))
+    for copy in writes:
         copy.start()
-    for read, write in zip(reads, writes):
-        read.wait()
-        write.start()
     for copy in writes:
         copy.wait()
 
@@ -601,8 +607,8 @@
     raw, chosen = pl.pallas_call(
         functools.partial(kernel, n),
         out_shape=(
-            jax.ShapeDtypeStruct((128, n * 256), BF),
-            jax.ShapeDtypeStruct(cache.shape, BF),
+            pltpu.VMEM((128, n * 256), BF),
+            pltpu.VMEM(cache.shape, BF),
         ),
         in_specs=[hbm] * 10,
         out_specs=(hbm, hbm),
@@ -623,6 +629,7 @@
             pltpu.VMEM((3, 128, 256), F32),
             pltpu.VMEM((PACKED, 128), F32),
             pltpu.VMEM((n, PACKED, 128), F32),
+            pltpu.VMEM((ROWS + 144, 256), BF),
             pltpu.VMEM((256, tokens), BF),
             pltpu.VMEM((768, 256), BF),
             pltpu.VMEM((3, 256, 128), F32),
@@ -671,12 +678,11 @@
         ),
         in_specs=[hbm] * 2,
         out_specs=(hbm, hbm),
-        scratch_shapes=[
-            pltpu.VMEM(raw.shape, BF),
-            pltpu.VMEM(cache.shape, BF),
-            dma((2, 2, 4)),
-        ],
-    )(raw, chosen)
+        scratch_shapes=[dma((2, 4))],
+    )(
+        pltpu.with_memory_space_constraint(raw, pltpu.VMEM),
+        pltpu.with_memory_space_constraint(chosen, pltpu.VMEM),
+    )
     return (attended[None, None], cache_after[None, None])
 
 

time: 40 us -> 37.1 us (0.927)
  Pallas kernels: 39.2 us -> 36.3 us
    pallas_call x1, Pallas kernels: 37 us -> 35.1 us  [shards(): pl.pallas_call(functools.partial(kernel, n), out_shape=(pltpu.VMEM((128,...]
    pallas_call x1, Pallas kernels: 2.22 us -> 1.2 us  [shards(): pl.pallas_call(place, out_shape=(jax.ShapeDtypeStruct(raw.shape, BF), jax...]
where the time goes in v5:
time: 37.1 us; the launch traced here: 36.9 us
  Pallas kernels  36.3 us (98%)
  between operations  0.64 us (2%)
    pallas_call x1, Pallas kernels, shards(): pl.pallas_call(functools.partial(kernel, n), out_shape=(pltpu.VMEM((128,...  35.1 us
    pallas_call x1, Pallas kernels, shards(): pl.pallas_call(place, out_shape=(jax.ShapeDtypeStruct(raw.shape, BF), jax...  1.2 us

profile of v5, /device:TPU:32, one launch (start us, length us, event | category | flops | bytes accessed | tf_op | source)
XLA Modules:
  0.0 36.9 jit_solution(5816033500118807733)
XLA Ops:
  0.6 35.1 %shard_map.113 = (bf16[128,4096]{1,0:T(8,128)(2,1)S(1)}, bf16[512,2,256]{2,1,0:T(2,128)(2,1)S(1)}) custom-call(s32[2,2]{1,0:T(2,128)} %crossing_hbm.1, s32[2,4]{1,0:T(2,128)} %lengths_hbm.1, s32[2,4]{1,0:T(2,128)} %steps_hbm.1, bf16[64,128]{1,0:T(8,128)(2,1)} %bitcast.16, f32[1,5120]{1,0:T(1,128)} %b_hbm.1, f32[2,256]{1,0:T(2,128)} %bitcast.17, ...), custom_call_target="tpu_custom_call" | custom-call | tf_op jit(solution)/shard_map/pallas_call | solution.py:607
  35.7 1.2 %shard_map.114 = (bf16[128,4096]{1,0:T(8,128)(2,1)}, bf16[512,2,256]{2,1,0:T(2,128)(2,1)}) custom-call(bf16[128,4096]{1,0:T(8,128)(2,1)S(1)} %get-tuple-element.6.raw, bf16[512,2,256]{2,1,0:T(2,128)(2,1)S(1)} %get-tuple-element.7.cache), custom_call_target="tpu_custom_call" | custom-call | tf_op jit(solution)/shard_map/pallas_call | solution.py:673

commit v6 on v5

--- a/solution.py
+++ b/solution.py
@@ -15,7 +15,7 @@
 F32 = jnp.float32
 MESH = pl.DeviceIdType.MESH
 ROWS = 80
-PACKED = 40
+PACKED = 48
 SIDE = 4
 QB = 512
 KB = 256
@@ -76,6 +76,7 @@
     xall,
     m_v,
     gbuf,
+    rest,
     g_in,
     stat,
     z2,
@@ -206,16 +207,14 @@
         return carry
 
     ld_x.wait()
-    pl.semaphore_wait(barrier, n - 1 + 4 + e)
 
     @pl.when(e == 0)
     def _():
+        pl.semaphore_wait(barrier, n - 1 + 4)
         for dst in range(4):
             z_copy(g, dst).start()
         xall[s] = x_v[...]
         lax.fori_loop(1, n, x_start, 0)
-        for dst in range(2):
-            cache_copy(half, dst).start()
 
     for copy in ld_scalars:
         copy.wait()
@@ -272,14 +271,17 @@
     at_col = lax.broadcasted_iota(jnp.int32, (64, 64), 1)
     core_q = gram_q[0:64, 0:64]
     core_k = gram_k[0:64, 0:64]
-    both = jnp.where(at_col < at_row, 2.0 * core_q, jnp.where(at_col == at_row, core_q, 2.0 * core_k))
-    gbuf[...] = jnp.zeros_like(gbuf)
+    both = jnp.where(at_col < at_row, 2.0 * core_q, jnp.where(at_col > at_row, 2.0 * core_k, 0.0)).astype(BF)
     gbuf[0:32, 0:64] = both[0:32, :]
     gbuf[0:32, 64:128] = both[32:64, :]
-    for at, values in enumerate((gram_q, gram_k)):
-        gbuf[32:34, at * 64 : at * 64 + 64] = values[64:66, 0:64]
-        gbuf[35 + 2 * at : 37 + 2 * at, 0:16] = values[64:66, 64:80]
-    gbuf[34:35, 0:64] = jnp.sum(jnp.where(at_col == at_row, core_k, 0.0), axis=0, keepdims=True)
+    rest[...] = jnp.zeros_like(rest)
+    for at, (values, centre) in enumerate(((gram_q, core_q), (gram_k, core_k))):
+        cols = slice(at * 64, at * 64 + 64)
+        rest[0:2, cols] = values[64:66, 0:64]
+        rest[2:3, cols] = jnp.sum(jnp.where(at_col == at_row, centre, 0.0), axis=0, keepdims=True)
+        rest[3 + 2 * at : 5 + 2 * at, 0:16] = values[64:66, 64:80]
+    hi, lo = split(rest[...])
+    gbuf[32:48, :] = jnp.concatenate([hi.astype(F32), lo.astype(F32)], axis=0).astype(BF)
 
     def g_copy(peer, slot):
         return pltpu.make_async_remote_copy(
@@ -305,7 +307,17 @@
         g_copy(lax.rem(s + k, n), s).start()
         return carry
 
+    @pl.when(e == 1)
+    def _():
+        pl.semaphore_wait(barrier, n - 1 + 4 + 1)
+
     lax.fori_loop(1, n, g_start, 0)
+
+    @pl.when(e == 0)
+    def _():
+        for dst in range(2):
+            cache_copy(half, dst).start()
+
 
     @pl.when(e == 1)
     def _():
@@ -371,17 +383,21 @@
     stat[0:ROWS, 0:ROWS] = hi
     stat[0:ROWS, 128 : 128 + ROWS] = lo
     g_all().wait_recv()
-    packed = g_in[0]
+    packed = g_in[0].astype(F32)
     for src in range(1, n):
-        packed = packed + g_in[src]
+        packed = packed + g_in[src].astype(F32)
     both = jnp.concatenate([packed[0:32, 0:64], packed[0:32, 64:128]], axis=0)
-    lower = jnp.where(at_col <= at_row, both, 0.0)
-    diagonal = jnp.where(at_col == at_row, jnp.broadcast_to(packed[34:35, 0:64], (64, 64)), 0.0)
-    upper = jnp.where(at_col > at_row, both, diagonal)
+    packed = packed[32:40, :] + packed[40:48, :]
+    diagonals = [
+        jnp.where(at_col == at_row, jnp.broadcast_to(packed[2:3, j * 64 : j * 64 + 64], (64, 64)), 0.0)
+        for j in range(2)
+    ]
+    lower = jnp.where(at_col < at_row, both, diagonals[0])
+    upper = jnp.where(at_col > at_row, both, diagonals[1])
     tail16 = lax.broadcasted_iota(jnp.int32, (16, 64), 0)
     linear = jnp.zeros((16, 64), F32)
     for at, row in enumerate(
-        (packed[32:33, 0:64], packed[33:34, 0:64], packed[32:33, 64:128], packed[33:34, 64:128])
+        (packed[0:1, 0:64], packed[1:2, 0:64], packed[0:1, 64:128], packed[1:2, 64:128])
     ):
         linear = jnp.where(tail16 == at, jnp.broadcast_to(row, (16, 64)), linear)
     hi, lo = split(jnp.concatenate([lower, upper, linear], axis=0))
@@ -405,7 +421,7 @@
         base = ROWS + 128 + 2 * j
         by_bias = t[base : base + 1, :]
         by_shift = t[base + 1 : base + 2, :]
-        at = 35 + 2 * j
+        at = 3 + 2 * j
         total = (
             rstd * rstd * (quad + 2.0 * by_bias + packed[at : at + 1, 0:1])
             + 2.0 * rstd * (by_shift + packed[at : at + 1, 1:2])
@@ -627,8 +643,9 @@
             pltpu.VMEM((4, 64, 128), BF),
             pltpu.VMEM((n, 64, 128), BF),
             pltpu.VMEM((3, 128, 256), F32),
-            pltpu.VMEM((PACKED, 128), F32),
-            pltpu.VMEM((n, PACKED, 128), F32),
+            pltpu.VMEM((PACKED, 128), BF),
+            pltpu.VMEM((8, 128), F32),
+            pltpu.VMEM((n, PACKED, 128), BF),
             pltpu.VMEM((ROWS + 144, 256), BF),
             pltpu.VMEM((256, tokens), BF),
             pltpu.VMEM((768, 256), BF),

time: 37.1 us -> 35.9 us (0.968)
  Pallas kernels: 36.3 us -> 35.1 us
    pallas_call x1, Pallas kernels: 35.1 us -> 33.9 us  [shards(): pl.pallas_call(functools.partial(kernel, n), out_shape=(pltpu.VMEM((128,...]
where the time goes in v6:
time: 35.9 us; the launch traced here: 35.7 us
  Pallas kernels  35.1 us (98%)
  between operations  0.64 us (2%)
    pallas_call x1, Pallas kernels, shards(): pl.pallas_call(functools.partial(kernel, n), out_shape=(pltpu.VMEM((128,...  33.9 us
    pallas_call x1, Pallas kernels, shards(): pl.pallas_call(place, out_shape=(jax.ShapeDtypeStruct(raw.shape, BF), jax...  1.2 us

profile of v6, /device:TPU:32, one launch (start us, length us, event | category | flops | bytes accessed | tf_op | source)
XLA Modules:
  0.0 35.7 jit_solution(10766994999290280610)
XLA Ops:
  0.6 33.9 %shard_map.113 = (bf16[128,4096]{1,0:T(8,128)(2,1)S(1)}, bf16[512,2,256]{2,1,0:T(2,128)(2,1)S(1)}) custom-call(s32[2,2]{1,0:T(2,128)} %crossing_hbm.1, s32[2,4]{1,0:T(2,128)} %lengths_hbm.1, s32[2,4]{1,0:T(2,128)} %steps_hbm.1, bf16[64,128]{1,0:T(8,128)(2,1)} %bitcast.16, f32[1,5120]{1,0:T(1,128)} %b_hbm.1, f32[2,256]{1,0:T(2,128)} %bitcast.17, ...), custom_call_target="tpu_custom_call" | custom-call | tf_op jit(solution)/shard_map/pallas_call | solution.py:623
  34.5 1.2 %shard_map.114 = (bf16[128,4096]{1,0:T(8,128)(2,1)}, bf16[512,2,256]{2,1,0:T(2,128)(2,1)}) custom-call(bf16[128,4096]{1,0:T(8,128)(2,1)S(1)} %get-tuple-element.6.raw, bf16[512,2,256]{2,1,0:T(2,128)(2,1)S(1)} %get-tuple-element.7.cache), custom_call_target="tpu_custom_call" | custom-call | tf_op jit(solution)/shard_map/pallas_call | solution.py:690

commit v7 on v6

--- a/solution.py
+++ b/solution.py
@@ -202,9 +202,9 @@
             device_id_type=MESH,
         )
 
-    def x_start(k, carry):
-        x_copy(lax.rem(s + k, n), s).start()
-        return carry
+    def x_start():
+        for peer in order[: n - 1]:
+            x_copy(peer, s).start()
 
     ld_x.wait()
 
@@ -214,7 +214,7 @@
         for dst in range(4):
             z_copy(g, dst).start()
         xall[s] = x_v[...]
-        lax.fori_loop(1, n, x_start, 0)
+        x_start()
 
     for copy in ld_scalars:
         copy.wait()
@@ -303,15 +303,15 @@
             device_id_type=MESH,
         )
 
-    def g_start(k, carry):
-        g_copy(lax.rem(s + k, n), s).start()
-        return carry
+    def g_start():
+        for peer in order[: n - 1]:
+            g_copy(peer, s).start()
 
     @pl.when(e == 1)
     def _():
         pl.semaphore_wait(barrier, n - 1 + 4 + 1)
 
-    lax.fori_loop(1, n, g_start, 0)
+    g_start()
 
     @pl.when(e == 0)
     def _():
@@ -324,7 +324,7 @@
         for src in range(4):
             z_copy(src, 0).wait_recv()
         xall[s] = jnp.where(arrived, zin[source], x_v[...])
-        lax.fori_loop(1, n, x_start, 0)
+        x_start()
 
     g_in[s] = gbuf[...]
 

time: 35.9 us -> 35.3 us (0.983)
  Pallas kernels: 35.1 us -> 34.2 us
    pallas_call x1, Pallas kernels: 33.9 us -> 33 us  [shards(): pl.pallas_call(functools.partial(kernel, n), out_shape=(pltpu.VMEM((128,...]
where the time goes in v7:
time: 35.3 us; the launch traced here: 34.9 us
  Pallas kernels  34.2 us (97%)
  between operations  0.64 us (2%)
    pallas_call x1, Pallas kernels, shards(): pl.pallas_call(functools.partial(kernel, n), out_shape=(pltpu.VMEM((128,...  33 us
    pallas_call x1, Pallas kernels, shards(): pl.pallas_call(place, out_shape=(jax.ShapeDtypeStruct(raw.shape, BF), jax...  1.2 us

profile of v7, /device:TPU:32, one launch (start us, length us, event | category | flops | bytes accessed | tf_op | source)
XLA Modules:
  0.0 34.9 jit_solution(11748923902631367136)
XLA Ops:
  0.6 33.0 %shard_map.113 = (bf16[128,4096]{1,0:T(8,128)(2,1)S(1)}, bf16[512,2,256]{2,1,0:T(2,128)(2,1)S(1)}) custom-call(s32[2,2]{1,0:T(2,128)} %crossing_hbm.1, s32[2,4]{1,0:T(2,128)} %lengths_hbm.1, s32[2,4]{1,0:T(2,128)} %steps_hbm.1, bf16[64,128]{1,0:T(8,128)(2,1)} %bitcast.16, f32[1,5120]{1,0:T(1,128)} %b_hbm.1, f32[2,256]{1,0:T(2,128)} %bitcast.17, ...), custom_call_target="tpu_custom_call" | custom-call | tf_op jit(solution)/shard_map/pallas_call | solution.py:623
  33.7 1.2 %shard_map.114 = (bf16[128,4096]{1,0:T(8,128)(2,1)}, bf16[512,2,256]{2,1,0:T(2,128)(2,1)}) custom-call(bf16[128,4096]{1,0:T(8,128)(2,1)S(1)} %get-tuple-element.6.raw, bf16[512,2,256]{2,1,0:T(2,128)(2,1)S(1)} %get-tuple-element.7.cache), custom_call_target="tpu_custom_call" | custom-call | tf_op jit(solution)/shard_map/pallas_call | solution.py:690

commit v8 on v7

--- a/solution.py
+++ b/solution.py
@@ -18,7 +18,7 @@
 PACKED = 48
 SIDE = 4
 QB = 512
-KB = 256
+KB = 512
 OWNERS = QB // 128
 STEPS = (
     ((2, 2), (1, 1), (3, 3), (2, 0))
@@ -138,15 +138,12 @@
 
     barrier = pltpu.get_barrier_semaphore()
 
-    def greet(k, carry):
-        pl.semaphore_signal(barrier, inc=1, device_id={"seq": lax.rem(s + k, n)}, device_id_type=MESH)
-        return carry
-
     for other in range(4):
         pl.semaphore_signal(
             barrier, inc=1, device_id={"expert": 1 - e, "group": other}, device_id_type=MESH
         )
-    lax.fori_loop(1, n, greet, 0)
+    for peer in order[: n - 1]:
+        pl.semaphore_signal(barrier, inc=1, device_id={"seq": peer}, device_id_type=MESH)
 
     @pl.when(e == 1)
     def _():

time: 35.3 us -> 35.5 us (level)
  no operation moved by 1% of the time
where the time goes in v8:
time: 35.5 us; the launch traced here: 35 us
  Pallas kernels  34.2 us (96%)
  between operations  0.8 us (2%)
    pallas_call x1, Pallas kernels, shards(): pl.pallas_call(functools.partial(kernel, n), out_shape=(pltpu.VMEM((128,...  33 us
    pallas_call x1, Pallas kernels, shards(): pl.pallas_call(place, out_shape=(jax.ShapeDtypeStruct(raw.shape, BF), jax...  1.2 us

profile of v8, /device:TPU:32, one launch (start us, length us, event | category | flops | bytes accessed | tf_op | source)
XLA Modules:
  0.0 35.0 jit_solution(16043995814258603615)
XLA Ops:
  0.6 33.0 %shard_map.113 = (bf16[128,4096]{1,0:T(8,128)(2,1)S(1)}, bf16[512,2,256]{2,1,0:T(2,128)(2,1)S(1)}) custom-call(s32[2,2]{1,0:T(2,128)} %crossing_hbm.1, s32[2,4]{1,0:T(2,128)} %lengths_hbm.1, s32[2,4]{1,0:T(2,128)} %steps_hbm.1, bf16[64,128]{1,0:T(8,128)(2,1)} %bitcast.16, f32[1,5120]{1,0:T(1,128)} %b_hbm.1, f32[2,256]{1,0:T(2,128)} %bitcast.17, ...), custom_call_target="tpu_custom_call" | custom-call | tf_op jit(solution)/shard_map/pallas_call | solution.py:620
  33.7 1.2 %shard_map.114 = (bf16[128,4096]{1,0:T(8,128)(2,1)}, bf16[512,2,256]{2,1,0:T(2,128)(2,1)}) custom-call(bf16[128,4096]{1,0:T(8,128)(2,1)S(1)} %get-tuple-element.6.raw, bf16[512,2,256]{2,1,0:T(2,128)(2,1)S(1)} %get-tuple-element.7.cache), custom_call_target="tpu_custom_call" | custom-call | tf_op jit(solution)/shard_map/pallas_call | solution.py:687
